TPU v7x, 32 devices: a whole 2x2x4 slice. The times are simulated.
32 devices in a mesh: groups: 2 (over y), blk: 8 (over z, x), rhs: 2 (over core).
Axes of the slice: x: 2, y: 2, z: 4, core: 2. Of those that a mesh axis runs over, the one named last changes fastest.
Arguments:
- forward: bfloat16 [128, 32, 256], P(('groups', 'blk'), 'rhs'), parts along dimension 0, may hold values from -6 to 6
- adjoint: bfloat16 [128, 32, 256], P(('groups', 'blk'), 'rhs'), parts along dimension 0, may hold values from -6 to 6
- row_home: int32 [128], P('groups'), parts along dimension 0, may hold values from 0 to 63, as said below
- block_rows: int32 [2, 512], P(None, ('groups', 'blk')), parts along dimension 1, may hold values from 0 to 63, as said below
- block_cols: int32 [2, 512], P(None, ('groups', 'blk')), parts along dimension 1, may hold values from 0 to 63, as said below
Outputs:
- grads: bfloat16 [2, 512, 256, 256], P(None, ('groups', 'blk'), 'rhs'), parts along dimension 1
There are 2 independent parts, one for each index of `groups`. A program takes and returns all parts, laid end to end along the dimension named above; each array names one. Nothing has to cross between parts.
Inputs may be any that keep to these rules, and one draw needn't show every extreme that they name: `row_home`: a permutation: each slot holds exactly one row block; the slot's holder along blk is its slot // 8. `block_rows`: within one device's entries of both strips together (64), at most 8 name row blocks held by any one device, and exactly 8 for some holder. `block_cols`: within one device's entries of both strips together (64), at most 8 name row blocks held by any one device, and exactly 8 for some holder.
All inputs are finite; a program needn't handle non-finite values.
Results may differ from a plain program's by a relative error of at most 0.001.
Values may be sent and summed in bfloat16 or wider, within the bound.
No kernel may reach another device: no remote copies, remote signals or barrier semaphores. Data moves between devices by JAX's collectives and lax.ppermute only.
A program may use at most 64 MiB of HBM per device.

v0:
```python
import jax
import jax.numpy as jnp
from jax import lax
from jax.sharding import PartitionSpec as P


def placing(blocks, row_home, stored, owners, capacity):
    slot_of = jnp.take(row_home, blocks)
    owner = slot_of // stored
    local = slot_of % stored
    order = jnp.arange(blocks.shape[0])
    earlier = (owner[:, None] == owner[None, :]) & (order[None, :] < order[:, None])
    rank = jnp.sum(earlier.astype(jnp.int32), axis=1)
    place = owner * capacity + rank
    targets = jnp.arange(owners * capacity)
    table = jnp.sum(jnp.where(place[:, None] == targets[None, :], local[:, None], 0), axis=0)
    return (table.reshape(owners, capacity), place)


def fetch(row_table, col_table, left_source, right_source):
    left = jnp.take(
        left_source,
        lax.all_to_all(row_table, "blk", split_axis=0, concat_axis=0, tiled=True),
        axis=0,
    )
    right = jnp.take(
        right_source,
        lax.all_to_all(col_table, "blk", split_axis=0, concat_axis=0, tiled=True),
        axis=0,
    )
    return (
        lax.all_to_all(left, "blk", split_axis=0, concat_axis=0, tiled=True),
        lax.all_to_all(right, "blk", split_axis=0, concat_axis=0, tiled=True),
    )


def select(fetched, place):
    flat = fetched.reshape((-1,) + fetched.shape[2:])
    return jnp.take(flat, place, axis=0)


def finish(left, right, half_start, half_width):
    left, right = (
        lax.all_gather(left, "rhs", axis=1, tiled=True),
        lax.all_gather(right, "rhs", axis=1, tiled=True),
    )
    left = lax.dynamic_slice_in_dim(left, half_start, half_width, 2)
    product = jnp.einsum("kra,krb->kab", left, right, preferred_element_type=jnp.float32)
    return (-product).astype(jnp.bfloat16)


def body(forward, adjoint, row_home, block_rows, block_cols):
    owners = lax.axis_size("blk")
    stored = forward.shape[0]
    slot_count = block_rows.shape[1]
    capacity = (2 * slot_count + owners - 1) // owners
    width = forward.shape[2]
    half_width = width // 2
    half_start = lax.axis_index("rhs") * half_width
    left_source, right_source = (adjoint, forward)
    row_table, row_place = placing(block_rows.reshape(-1), row_home, stored, owners, capacity)
    col_table, col_place = placing(block_cols.reshape(-1), row_home, stored, owners, capacity)
    left_all, right_all = fetch(row_table, col_table, left_source, right_source)
    result = finish(
        select(left_all, row_place), select(right_all, col_place), half_start, half_width
    )
    return result.reshape(2, slot_count, half_width, width)


def solution(mesh):
    placed = (
        P(("groups", "blk"), "rhs", None),
        P(("groups", "blk"), "rhs", None),
        P("groups"),
        P(None, ("groups", "blk")),
        P(None, ("groups", "blk")),
    )
    return jax.shard_map(
        body,
        mesh=mesh,
        in_specs=placed,
        out_specs=P(None, ("groups", "blk"), "rhs", None),
        check_vma=False,
    )
```

profile of v0, /device:TPU:0, one launch (start us, length us, event | category | flops | bytes accessed | tf_op | source)
XLA Modules:
  0.0 88.7 jit_solution(3960111840743186624)
XLA Ops:
  6.5 0.0 copy-start
  6.5 0.0 copy-start.1
  6.5 0.8 reshape.46
  7.3 1.4 %gather_fusion = s32[64]{0:T(128)S(1)} fusion(s32[64]{0:T(128)} %param.13, s32[1024]{0:T(1024)S(1)} %pad_clamp_fusion.5), kind=kCustom, calls=%fused_computation.clone | custom fusion | bytes 768 | tf_op jit(solution)/shard_map/jit(_take)/gather | solution.py:8
  8.8 0.2 convert_reduce_fusion.1
  9.0 0.1 select_reduce_fusion.1
  9.1 0.7 all_to_all.22
  9.8 7.3 %all-to-all-start = ((s32[8,1,8]{2,1,0:T(1,128)}), s32[8,1,8]{2,1,0:T(1,128)S(1)}, u32[]{:S(2)}, u32[]{:S(2)}) async-start(s32[8,1,8]{2,1,0:T(1,128)} %bitcast), calls=%async_computation | async-start | bytes 8192 | tf_op jit(solution)/shard_map/all_to_all | solution.py:23
  17.0 0.8 reshape.48
  17.8 1.4 %gather_fusion.3 = s32[64]{0:T(128)S(1)} fusion(s32[64]{0:T(128)} %param.13, s32[1024]{0:T(1024)S(1)} %pad_clamp_fusion.2), kind=kCustom, calls=%fused_computation.3.clone | custom fusion | bytes 768 | tf_op jit(solution)/shard_map/jit(_take)/gather | solution.py:8
  19.3 0.2 convert_reduce_fusion
  19.5 0.1 select_reduce_fusion
  19.6 0.7 all_to_all.26
  20.3 3.2 %all-to-all-done = s32[8,1,8]{2,1,0:T(1,128)S(1)} async-done(((s32[8,1,8]{2,1,0:T(1,128)}), s32[8,1,8]{2,1,0:T(1,128)S(1)}, u32[]{:S(2)}, u32[]{:S(2)}) %all-to-all-start) | async-done | bytes 288 | tf_op jit(solution)/shard_map/all_to_all | solution.py:23
  23.5 3.3 %all-to-all-start.2 = ((s32[8,1,8]{2,1,0:T(1,128)}), s32[8,1,8]{2,1,0:T(1,128)S(1)}, u32[]{:S(2)}, u32[]{:S(2)}) async-start(s32[8,1,8]{2,1,0:T(1,128)} %bitcast.4), calls=%async_computation.2 | async-start | bytes 8192 | tf_op jit(solution)/shard_map/all_to_all | solution.py:28
  26.9 0.1 reshape.109
  26.9 0.0 copy-done
  26.9 0.6 gather_fusion.1
  27.6 0.9 %broadcast_select_fusion.3 = bf16[8,8,16,256]{3,2,1,0:T(8,128)(2,1)} fusion(bf16[8,8,16,256]{3,2,1,0:T(8,128)(2,1)S(1)} %bitcast.11, pred[8,8]{1,0:T(8,128)(4,1)S(1)} %compare_and_fusion.1), kind=kLoop, calls=%fused_computation.11 | loop fusion | flops 262144 | bytes 1048640 | tf_op jit(solution)/shard_map/jit(_take)/select_n | solution.py:21
  28.5 4.7 %all-to-all-done.2 = s32[8,1,8]{2,1,0:T(1,128)S(1)} async-done(((s32[8,1,8]{2,1,0:T(1,128)}), s32[8,1,8]{2,1,0:T(1,128)S(1)}, u32[]{:S(2)}, u32[]{:S(2)}) %all-to-all-start.2) | async-done | bytes 288 | tf_op jit(solution)/shard_map/all_to_all | solution.py:28
  33.2 3.5 %all-to-all-start.1 = ((bf16[8,8,16,256]{3,2,1,0:T(8,128)(2,1)}), bf16[8,8,16,256]{3,2,1,0:T(8,128)(2,1)S(1)}, u32[]{:S(2)}, u32[]{:S(2)}) async-start(bf16[8,8,16,256]{3,2,1,0:T(8,128)(2,1)} %broadcast_select_fusion.3), calls=%async_computation.1 | async-start | bytes 1048576 | tf_op jit(solution)/shard_map/all_to_all | solution.py:32
  36.7 0.1 reshape.117
  36.8 0.0 copy-done.1
  36.8 0.6 gather_fusion.4
  37.4 0.9 %broadcast_select_fusion.2 = bf16[8,8,16,256]{3,2,1,0:T(8,128)(2,1)} fusion(bf16[8,8,16,256]{3,2,1,0:T(8,128)(2,1)S(1)} %bitcast.10, pred[8,8]{1,0:T(8,128)(4,1)S(1)} %compare_and_fusion), kind=kLoop, calls=%fused_computation.10 | loop fusion | flops 262144 | bytes 1048640 | tf_op jit(solution)/shard_map/jit(_take)/select_n | solution.py:26
  38.3 10.5 %all-to-all-done.1 = bf16[8,8,16,256]{3,2,1,0:T(8,128)(2,1)S(1)} async-done(((bf16[8,8,16,256]{3,2,1,0:T(8,128)(2,1)}), bf16[8,8,16,256]{3,2,1,0:T(8,128)(2,1)S(1)}, u32[]{:S(2)}, u32[]{:S(2)}) %all-to-all-start.1) | async-done | bytes 524320 | tf_op jit(solution)/shard_map/all_to_all | solution.py:32
  48.8 3.7 %all-to-all-start.3 = ((bf16[8,8,16,256]{3,2,1,0:T(8,128)(2,1)}), bf16[8,8,16,256]{3,2,1,0:T(8,128)(2,1)S(1)}, u32[]{:S(2)}, u32[]{:S(2)}) async-start(bf16[8,8,16,256]{3,2,1,0:T(8,128)(2,1)} %broadcast_select_fusion.2), calls=%async_computation.3 | async-start | bytes 1048576 | tf_op jit(solution)/shard_map/all_to_all | solution.py:33
  52.5 0.0 all-gather.3.cloned.1.call-start
  52.5 0.6 gather_fusion.2
  53.2 1.0 %broadcast_select_fusion.1 = bf16[64,16,256]{2,1,0:T(8,128)(2,1)} fusion(bf16[64,16,256]{2,1,0:T(8,128)(2,1)S(1)} %gather_fusion.2, pred[64]{0:T(512)(128)(4,1)S(1)} %get-tuple-element.6), kind=kLoop, calls=%fused_computation.9 | loop fusion | flops 262144 | bytes 1048640 | tf_op jit(solution)/shard_map/jit(_take)/select_n | solution.py:39
  54.1 0.0 all-gather.3.cloned.1.call-update
  54.1 0.0 all-gather.5.cloned.1.call-start
  54.2 11.5 %all-to-all-done.3 = bf16[8,8,16,256]{3,2,1,0:T(8,128)(2,1)S(1)} async-done(((bf16[8,8,16,256]{3,2,1,0:T(8,128)(2,1)}), bf16[8,8,16,256]{3,2,1,0:T(8,128)(2,1)S(1)}, u32[]{:S(2)}, u32[]{:S(2)}) %all-to-all-start.3) | async-done | bytes 524320 | tf_op jit(solution)/shard_map/all_to_all | solution.py:33
  65.7 0.6 gather_fusion.5
  66.3 0.9 %broadcast_select_fusion = bf16[64,16,256]{2,1,0:T(8,128)(2,1)} fusion(bf16[64,16,256]{2,1,0:T(8,128)(2,1)S(1)} %gather_fusion.5, pred[64]{0:T(512)(128)(4,1)S(1)} %get-tuple-element.12), kind=kLoop, calls=%fused_computation.8 | loop fusion | flops 262144 | bytes 1048640 | tf_op jit(solution)/shard_map/jit(_take)/select_n | solution.py:39
  67.3 0.0 all-gather.5.cloned.1.call-update
  67.3 0.0 all-gather.3.cloned.1.call-done
  67.3 9.8 %all-gather.5.cloned.1.call-done = bf16[64,32,256]{2,1,0:T(8,128)(2,1)} async-done(((bf16[64,16,256]{2,1,0:T(8,128)(2,1)}), bf16[64,32,256]{2,1,0:T(8,128)(2,1)}) %all-gather.5.cloned.1.call-update) | async-done | bytes 1048592 | tf_op jit(solution)/shard_map/all_gather | solution.py:45
  77.2 4.7 %negate_convert_fusion = bf16[64,128,256]{2,1,0:T(8,128)(2,1)} fusion(bf16[64,32,256]{2,1,0:T(8,128)(2,1)} %all-gather.5.cloned.1.call-done, bf16[64,32,256]{2,1,0:T(8,128)(2,1)} %all-gather.3.cloned.1.call-done, s32[]{:T(128)S(6)} %select_n.51), kind=kOutput, calls=%fused_computation.6 | convolution fusion | flops 138412032 | bytes 5767172 | tf_op jit(solution)/shard_map/kra,krb->kab/dot_general | solution.py:48
  (20 shorter events, 0.2 us)
Async XLA Ops:
  6.5 20.4 %copy-start = (bf16[8,16,256]{2,1,0:T(8,128)(2,1)S(1)}, bf16[8,16,256]{2,1,0:T(8,128)(2,1)}, u32[]{:S(2)}) copy-start(bf16[8,16,256]{2,1,0:T(8,128)(2,1)} %param.12) | copy-start | bytes 196612
  6.5 30.2 %copy-start.1 = (bf16[8,16,256]{2,1,0:T(8,128)(2,1)S(1)}, bf16[8,16,256]{2,1,0:T(8,128)(2,1)}, u32[]{:S(2)}) copy-start(bf16[8,16,256]{2,1,0:T(8,128)(2,1)} %param.11) | copy-start | bytes 196612
  9.8 13.7 %all-to-all-start = ((s32[8,1,8]{2,1,0:T(1,128)}), s32[8,1,8]{2,1,0:T(1,128)S(1)}, u32[]{:S(2)}, u32[]{:S(2)}) async-start(s32[8,1,8]{2,1,0:T(1,128)} %bitcast), calls=%async_computation | async-start | bytes 8192 | tf_op jit(solution)/shard_map/all_to_all | solution.py:23
  23.5 9.6 %all-to-all-start.2 = ((s32[8,1,8]{2,1,0:T(1,128)}), s32[8,1,8]{2,1,0:T(1,128)S(1)}, u32[]{:S(2)}, u32[]{:S(2)}) async-start(s32[8,1,8]{2,1,0:T(1,128)} %bitcast.4), calls=%async_computation.2 | async-start | bytes 8192 | tf_op jit(solution)/shard_map/all_to_all | solution.py:28
  33.2 15.7 %all-to-all-start.1 = ((bf16[8,8,16,256]{3,2,1,0:T(8,128)(2,1)}), bf16[8,8,16,256]{3,2,1,0:T(8,128)(2,1)S(1)}, u32[]{:S(2)}, u32[]{:S(2)}) async-start(bf16[8,8,16,256]{3,2,1,0:T(8,128)(2,1)} %broadcast_select_fusion.3), calls=%async_computation.1 | async-start | bytes 1048576 | tf_op jit(solution)/shard_map/all_to_all | solution.py:32
  48.8 16.9 %all-to-all-start.3 = ((bf16[8,8,16,256]{3,2,1,0:T(8,128)(2,1)}), bf16[8,8,16,256]{3,2,1,0:T(8,128)(2,1)S(1)}, u32[]{:S(2)}, u32[]{:S(2)}) async-start(bf16[8,8,16,256]{3,2,1,0:T(8,128)(2,1)} %broadcast_select_fusion.2), calls=%async_computation.3 | async-start | bytes 1048576 | tf_op jit(solution)/shard_map/all_to_all | solution.py:33
  52.5 14.8 %all-gather.3.cloned.1.call-start = ((), (), s32[]{:S(2)}) async-start(), calls=%async_computation.4 | async-start | bytes 1572864 | tf_op jit(solution)/shard_map/all_gather | solution.py:44
  54.1 23.0 %all-gather.5.cloned.1.call-start = ((), (), s32[]{:S(2)}) async-start(), calls=%async_computation.5 | async-start | bytes 1572864 | tf_op jit(solution)/shard_map/all_gather | solution.py:45
Sparse Core Ops, SparseCore 0:
  54.9 10.4 all-gather.2
  67.4 9.6 all-gather.4
where the time goes:
time: 89.2 us; the launch traced here: 88.7 us
  waiting for transfers between devices  39.8 us (45%)
  starting transfers between devices  17.8 us (20%)
  between operations  13.6 us (15%)
  local copies, waits for them, and re-layouts  8.32 us (9%)
  matrix products  4.7 us (5%)
  other arithmetic  4.47 us (5%)
    all_to_all x1, waiting for transfers between devices, fetch(): lax.all_to_all(right, 'blk', split_axis=0, concat_axis=0, tiled=True)  11.5 us
    all_to_all x1, waiting for transfers between devices, fetch(): lax.all_to_all(left, 'blk', split_axis=0, concat_axis=0, tiled=True)  10.5 us
    all_gather x1, waiting for transfers between devices, finish(): lax.all_gather(right, 'rhs', axis=1, tiled=True)  9.82 us
    all_to_all x1, starting transfers between devices, fetch(): lax.all_to_all(row_table, 'blk', split_axis=0, concat_axis=0, tiled=True)  7.25 us
    dot_general x1, matrix products, finish(): jnp.einsum('kra,krb->kab', left, right, preferred_element_type=jnp.float32)  4.7 us
    all_to_all x1, waiting for transfers between devices, fetch(): lax.all_to_all(col_table, 'blk', split_axis=0, concat_axis=0, tiled=True)  4.66 us
    all_to_all x1, starting transfers between devices, fetch(): lax.all_to_all(right, 'blk', split_axis=0, concat_axis=0, tiled=True)  3.65 us
    all_to_all x1, starting transfers between devices, fetch(): lax.all_to_all(left, 'blk', split_axis=0, concat_axis=0, tiled=True)  3.49 us
  transfers between devices with their start and end apart: 6, of which 5 were waited for; matrix products, arithmetic and copies ran while one was open for 10% of the time, Pallas kernels for 0%

commit v1 on v0

--- a/solution.py
+++ b/solution.py
@@ -1,7 +1,16 @@
+import functools
+
 import jax
 import jax.numpy as jnp
 from jax import lax
+from jax.experimental import pallas as pl
+from jax.experimental.pallas import tpu as pltpu
 from jax.sharding import PartitionSpec as P
+
+STEP = 8
+ANY = pl.BlockSpec(memory_space=pl.ANY)
+SMEM = pl.BlockSpec(memory_space=pltpu.SMEM)
+VMEM = pl.BlockSpec(memory_space=pltpu.VMEM)
 
 
 def placing(blocks, row_home, stored, owners, capacity):
@@ -49,7 +58,7 @@
     return (-product).astype(jnp.bfloat16)
 
 
-def body(forward, adjoint, row_home, block_rows, block_cols):
+def tabled(forward, adjoint, row_home, block_rows, block_cols):
     owners = lax.axis_size("blk")
     stored = forward.shape[0]
     slot_count = block_rows.shape[1]
@@ -67,6 +76,148 @@
     return result.reshape(2, slot_count, half_width, width)
 
 
+def join_kernel(a, b, out, sem):
+    n = a.shape[0]
+    copies = [
+        pltpu.make_async_copy(a, out.at[pl.ds(0, n)], sem.at[0]),
+        pltpu.make_async_copy(b, out.at[pl.ds(n, n)], sem.at[1]),
+    ]
+    for copy in copies:
+        copy.start()
+    for copy in copies:
+        copy.wait()
+
+
+def join(a, b):
+    return pl.pallas_call(
+        join_kernel,
+        out_shape=pltpu.VMEM((2 * a.shape[0],) + a.shape[1:], a.dtype),
+        in_specs=[ANY, ANY],
+        out_specs=ANY,
+        scratch_shapes=[pltpu.SemaphoreType.DMA((2,))],
+        compiler_params=pltpu.CompilerParams(vmem_limit_bytes=1 << 20),
+    )(*(pltpu.with_memory_space_constraint(v, pltpu.HBM) for v in (a, b)))
+
+
+def products_kernel(owners, stored, half, *refs):
+    mine, others = refs[:owners], refs[owners : 2 * owners]
+    home, rows, cols, out = refs[2 * owners : 2 * owners + 4]
+    home_s, rows_s, cols_s, left, right, result, in_sem, index_sem, out_sem = refs[2 * owners + 4 :]
+    start = pl.multiple_of(lax.axis_index("rhs") * half, half)
+    me = lax.axis_index("blk")
+    rhs = mine[0].shape[1]
+    copies = [
+        pltpu.make_async_copy(home, home_s, index_sem.at[0]),
+        pltpu.make_async_copy(rows, rows_s, index_sem.at[1]),
+        pltpu.make_async_copy(cols, cols_s, index_sem.at[2]),
+    ]
+    for j in range(owners):
+        slots = pl.ds(j * stored, stored)
+        for c, source in enumerate((mine[j], others[j])):
+            part = pl.ds(c * rhs, rhs)
+            copies.append(
+                pltpu.make_async_copy(
+                    source.at[pl.ds(0, stored)], right.at[slots, part], in_sem.at[c, 0, j]
+                )
+            )
+            copies.append(
+                pltpu.make_async_copy(
+                    source.at[pl.ds(stored, stored), :, pl.ds(start, half)],
+                    left.at[slots, part],
+                    in_sem.at[c, 1, j],
+                )
+            )
+    for copy in copies:
+        copy.start()
+    for copy in copies:
+        copy.wait()
+
+    _, per_strip = rows_s.shape
+    steps = result.shape[0] // STEP
+
+    def place(block):
+        slot = home_s[block]
+        owner = lax.div(slot, stored)
+        return jnp.bitwise_xor(owner, me) * stored + lax.rem(slot, stored)
+
+    def out_copy(step):
+        part = pl.ds(step * STEP, STEP)
+        return pltpu.make_async_copy(result.at[part], out.at[part], out_sem.at[step])
+
+    def one_step(step, carry):
+        strip, first = lax.div(step * STEP, per_strip), lax.rem(step * STEP, per_strip)
+        for k in range(STEP):
+            a = left[place(rows_s[strip, first + k])]
+            b = right[place(cols_s[strip, first + k])]
+            product = lax.dot_general(
+                -a, b, (((0,), (0,)), ((), ())), preferred_element_type=jnp.float32
+            )
+            result[step * STEP + k] = product.astype(jnp.bfloat16)
+        out_copy(step).start()
+        return carry
+
+    lax.fori_loop(0, steps, one_step, 0)
+
+    def drain(step, carry):
+        out_copy(step).wait()
+        return carry
+
+    lax.fori_loop(0, steps, drain, 0)
+
+
+def products(mine, others, row_home, block_rows, block_cols):
+    owners = len(mine)
+    joined, rhs, width = mine[0].shape
+    stored, half = joined // 2, width // 2
+    entries = block_rows.size
+    index = [
+        pltpu.with_memory_space_constraint(v, pltpu.HBM)
+        for v in (row_home, block_rows, block_cols)
+    ]
+    return pl.pallas_call(
+        functools.partial(products_kernel, owners, stored, half),
+        out_shape=jax.ShapeDtypeStruct((entries, half, width), jnp.bfloat16),
+        in_specs=[ANY] * (2 * owners + 3),
+        out_specs=ANY,
+        scratch_shapes=[
+            pltpu.SMEM(row_home.shape, jnp.int32),
+            pltpu.SMEM(block_rows.shape, jnp.int32),
+            pltpu.SMEM(block_cols.shape, jnp.int32),
+            pltpu.VMEM((owners * stored, 2 * rhs, half), jnp.bfloat16),
+            pltpu.VMEM((owners * stored, 2 * rhs, width), jnp.bfloat16),
+            pltpu.VMEM((entries, half, width), jnp.bfloat16),
+            pltpu.SemaphoreType.DMA((2, 2, owners)),
+            pltpu.SemaphoreType.DMA((3,)),
+            pltpu.SemaphoreType.DMA((entries // STEP,)),
+        ],
+        compiler_params=pltpu.CompilerParams(vmem_limit_bytes=24 << 20),
+    )(*mine, *others, *index)
+
+
+PLAN = ((4, 4), (3, 3), (2, 2), (1, 1), (7, 3), (6, 2), (5, 1))
+
+
+def gathered(forward, adjoint, row_home, block_rows, block_cols):
+    owners = lax.axis_size("blk")
+
+    def across(value, mask):
+        return lax.ppermute(value, "blk", [(i, i ^ mask) for i in range(owners)])
+
+    held = {0: join(forward, adjoint)}
+    for mask, via in PLAN:
+        held[mask] = across(held[mask ^ via], via)
+    mine = [held[j] for j in range(owners)]
+    others = [lax.ppermute(v, "rhs", [(0, 1), (1, 0)]) for v in mine]
+    result = products(mine, others, row_home, block_rows, block_cols)
+    return result.reshape(2, block_rows.shape[1], *result.shape[1:])
+
+
+def body(forward, adjoint, row_home, block_rows, block_cols):
+    if lax.axis_size("blk") == 8 and forward.shape[0] * 8 <= 2 * block_rows.shape[1]:
+        return gathered(forward, adjoint, row_home, block_rows, block_cols)
+    return tabled(forward, adjoint, row_home, block_rows, block_cols)
+
+
 def solution(mesh):
     placed = (
         P(("groups", "blk"), "rhs", None),

time: 89.2 us -> 28.6 us (0.32)
  waiting for transfers between devices: 39.8 us -> 11.1 us
  between operations: 13.6 us -> 0.03 us
  local copies, waits for them, and re-layouts: 8.32 us -> 0 us
  starting transfers between devices: 17.8 us -> 11.7 us
  Pallas kernels: 0 us -> 5.57 us
  matrix products: 4.7 us -> 0 us
  other arithmetic: 4.47 us -> 0 us
    all_to_all x4 -> x0, waiting for transfers between devices: 30 us -> none  [the longest x1 11.5 us: fetch(): lax.all_to_all(right, 'blk', split_axis=0, concat_axis=0, tiled=True)]
    all_to_all x4 -> x0, starting transfers between devices: 17.7 us -> none  [the longest x1 7.25 us: fetch(): lax.all_to_all(row_table, 'blk', split_axis=0, concat_axis=0, tiled=True)]
    ppermute x0 -> x15, starting transfers between devices: none -> 11.7 us  [the longest x7 10.7 us: across(): return lax.ppermute(value, 'blk', [(i, i ^ mask) for i in range(owners)])]
    ppermute x0 -> x15, waiting for transfers between devices: none -> 11.1 us  [the longest x7 9.81 us: across(): return lax.ppermute(value, 'blk', [(i, i ^ mask) for i in range(owners)])]
    all_gather x2 -> x0, waiting for transfers between devices: 9.84 us -> none  [the longest x1 9.82 us: finish(): lax.all_gather(right, 'rhs', axis=1, tiled=True)]
    pallas_call x0 -> x2, Pallas kernels: none -> 5.57 us  [the longest x1 4.68 us: products(): pl.pallas_call(functools.partial(products_kernel, owners, stored, half),...]
    gather x6 -> x0, local copies, waits for them, and re-layouts: 5.23 us -> none  [the longest x2 2.85 us: placing(): slot_of = jnp.take(row_home, blocks)]
    dot_general x1 -> x0, matrix products: 4.7 us -> none  [finish(): jnp.einsum('kra,krb->kab', left, right, preferred_element_type=jnp.float32)]
  transfers between devices with their start and end apart: 6 -> 15, of which waited for: 5 -> 8; matrix products, arithmetic and copies ran while one was open for 10% -> 0% of each run, Pallas kernels for 0% -> 0%
where the time goes in v1:
time: 28.6 us; the launch traced here: 28.4 us
  starting transfers between devices  11.7 us (41%)
  waiting for transfers between devices  11.1 us (39%)
  Pallas kernels  5.57 us (19%)
    ppermute x7, starting transfers between devices, across(): return lax.ppermute(value, 'blk', [(i, i ^ mask) for i in range(owners)])  10.7 us
    ppermute x7, waiting for transfers between devices, across(): return lax.ppermute(value, 'blk', [(i, i ^ mask) for i in range(owners)])  9.81 us
    pallas_call x1, Pallas kernels, products(): pl.pallas_call(functools.partial(products_kernel, owners, stored, half),...  4.68 us
    ppermute x8, waiting for transfers between devices, gathered(): others = [lax.ppermute(v, 'rhs', [(0, 1), (1, 0)]) for v in mine]  1.28 us
    ppermute x8, starting transfers between devices, gathered(): others = [lax.ppermute(v, 'rhs', [(0, 1), (1, 0)]) for v in mine]  1.05 us
    pallas_call x1, Pallas kernels, join(): pl.pallas_call(join_kernel, out_shape=pltpu.VMEM((2 * a.shape[0],) + a.sh...  0.89 us
  transfers between devices with their start and end apart: 15, of which 8 were waited for; matrix products, arithmetic and copies ran while one was open for 0% of the time, Pallas kernels for 0%

profile of v1, /device:TPU:0, one launch (start us, length us, event | category | flops | bytes accessed | tf_op | source)
XLA Modules:
  0.0 28.4 jit_solution(14420710041632501654)
XLA Ops:
  0.0 0.9 %shard_map.55.refs_0_ = bf16[16,16,256]{2,1,0:T(8,128)(2,1)S(1)} custom-call(bf16[8,16,256]{2,1,0:T(8,128)(2,1)} %a.1, bf16[8,16,256]{2,1,0:T(8,128)(2,1)} %b.1), custom_call_target="tpu_custom_call" | custom-call | tf_op jit(solution)/shard_map/pallas_call | solution.py:92
  0.9 4.1 %collective-permute-start.3 = (bf16[16,16,256]{2,1,0:T(8,128)(2,1)S(1)}, bf16[16,16,256]{2,1,0:T(8,128)(2,1)S(1)}, u32[]{:S(2)}, u32[]{:S(2)}) collective-permute-start(bf16[16,16,256]{2,1,0:T(8,128)(2,1)S(1)} %shard_map.55.refs_0_), channel_id=1, source_target_pairs={{0,8},{2,10},{4,12},{6,14},{8,0},{10,2},{12,4},{14,6},{1,9},{3,11}... | collective-permute-start | bytes 393224 | tf_op jit(solution)/shard_map/ppermute | solution.py:204
  5.0 0.0 collective-permute-start.7
  5.0 2.5 %collective-permute-start.2 = (bf16[16,16,256]{2,1,0:T(8,128)(2,1)S(1)}, bf16[16,16,256]{2,1,0:T(8,128)(2,1)S(1)}, u32[]{:S(2)}, u32[]{:S(2)}) collective-permute-start(bf16[16,16,256]{2,1,0:T(8,128)(2,1)S(1)} %shard_map.55.refs_0_), channel_id=1, source_target_pairs={{0,6},{2,4},{4,2},{6,0},{8,14},{10,12},{12,10},{14,8},{1,7},{3,5},... | collective-permute-start | bytes 393224 | tf_op jit(solution)/shard_map/ppermute | solution.py:204
  7.5 0.4 %collective-permute-start.1 = (bf16[16,16,256]{2,1,0:T(8,128)(2,1)S(1)}, bf16[16,16,256]{2,1,0:T(8,128)(2,1)S(1)}, u32[]{:S(2)}, u32[]{:S(2)}) collective-permute-start(bf16[16,16,256]{2,1,0:T(8,128)(2,1)S(1)} %shard_map.55.refs_0_), channel_id=1, source_target_pairs={{0,4},{2,6},{4,0},{6,2},{8,12},{10,14},{12,8},{14,10},{1,5},{3,7},... | collective-permute-start | bytes 393224 | tf_op jit(solution)/shard_map/ppermute | solution.py:204
  8.0 0.5 %collective-permute-start = (bf16[16,16,256]{2,1,0:T(8,128)(2,1)S(1)}, bf16[16,16,256]{2,1,0:T(8,128)(2,1)S(1)}, u32[]{:S(2)}, u32[]{:S(2)}) collective-permute-start(bf16[16,16,256]{2,1,0:T(8,128)(2,1)S(1)} %shard_map.55.refs_0_), channel_id=1, source_target_pairs={{0,2},{2,0},{4,6},{6,4},{8,10},{10,8},{12,14},{14,12},{1,3},{3,1},... | collective-permute-start | bytes 393224 | tf_op jit(solution)/shard_map/ppermute | solution.py:204
  8.5 2.9 %collective-permute-done.3.refs_4_ = bf16[16,16,256]{2,1,0:T(8,128)(2,1)S(1)} collective-permute-done((bf16[16,16,256]{2,1,0:T(8,128)(2,1)S(1)}, bf16[16,16,256]{2,1,0:T(8,128)(2,1)S(1)}, u32[]{:S(2)}, u32[]{:S(2)}) %collective-permute-start.3) | collective-permute-done | bytes 131104 | tf_op jit(solution)/shard_map/ppermute | solution.py:204
  11.4 0.0 collective-permute-start.11
  11.4 0.0 collective-permute-done.7.refs_8_
  11.4 1.6 %collective-permute-start.6 = (bf16[16,16,256]{2,1,0:T(8,128)(2,1)S(1)}, bf16[16,16,256]{2,1,0:T(8,128)(2,1)S(1)}, u32[]{:S(2)}, u32[]{:S(2)}) collective-permute-start(bf16[16,16,256]{2,1,0:T(8,128)(2,1)S(1)} %collective-permute-done.3.refs_4_), channel_id=1, source_target_pairs={{0,6},{2,4},{4,2},{6,0},{8,14},{10,12},{12,10},{14,8},{1,7},{3,5},... | collective-permute-start | bytes 393224 | tf_op jit(solution)/shard_map/ppermute | solution.py:204
  13.0 0.9 %collective-permute-done.2.refs_3_ = bf16[16,16,256]{2,1,0:T(8,128)(2,1)S(1)} collective-permute-done((bf16[16,16,256]{2,1,0:T(8,128)(2,1)S(1)}, bf16[16,16,256]{2,1,0:T(8,128)(2,1)S(1)}, u32[]{:S(2)}, u32[]{:S(2)}) %collective-permute-start.2) | collective-permute-done | bytes 131104 | tf_op jit(solution)/shard_map/ppermute | solution.py:204
  13.9 0.7 %collective-permute-start.5 = (bf16[16,16,256]{2,1,0:T(8,128)(2,1)S(1)}, bf16[16,16,256]{2,1,0:T(8,128)(2,1)S(1)}, u32[]{:S(2)}, u32[]{:S(2)}) collective-permute-start(bf16[16,16,256]{2,1,0:T(8,128)(2,1)S(1)} %collective-permute-done.3.refs_4_), channel_id=1, source_target_pairs={{0,4},{2,6},{4,0},{6,2},{8,12},{10,14},{12,8},{14,10},{1,5},{3,7},... | collective-permute-start | bytes 393224 | tf_op jit(solution)/shard_map/ppermute | solution.py:204
  14.6 1.9 %collective-permute-done.1.refs_2_ = bf16[16,16,256]{2,1,0:T(8,128)(2,1)S(1)} collective-permute-done((bf16[16,16,256]{2,1,0:T(8,128)(2,1)S(1)}, bf16[16,16,256]{2,1,0:T(8,128)(2,1)S(1)}, u32[]{:S(2)}, u32[]{:S(2)}) %collective-permute-start.1) | collective-permute-done | bytes 131104 | tf_op jit(solution)/shard_map/ppermute | solution.py:204
  16.5 0.8 %collective-permute-start.4 = (bf16[16,16,256]{2,1,0:T(8,128)(2,1)S(1)}, bf16[16,16,256]{2,1,0:T(8,128)(2,1)S(1)}, u32[]{:S(2)}, u32[]{:S(2)}) collective-permute-start(bf16[16,16,256]{2,1,0:T(8,128)(2,1)S(1)} %collective-permute-done.3.refs_4_), channel_id=1, source_target_pairs={{0,2},{2,0},{4,6},{6,4},{8,10},{10,8},{12,14},{14,12},{1,3},{3,1},... | collective-permute-start | bytes 393224 | tf_op jit(solution)/shard_map/ppermute | solution.py:204
  17.3 0.0 collective-permute-done.refs_1_
  17.3 0.0 collective-permute-start.10
  17.3 0.0 collective-permute-done.11.refs_12_
  17.3 0.5 %collective-permute-start.9 = (bf16[16,16,256]{2,1,0:T(8,128)(2,1)S(1)}, bf16[16,16,256]{2,1,0:T(8,128)(2,1)S(1)}, u32[]{:S(2)}, u32[]{:S(2)}) collective-permute-start(bf16[16,16,256]{2,1,0:T(8,128)(2,1)S(1)} %collective-permute-done.1.refs_2_), channel_id=1, source_target_pairs={{0,1},{1,0},{2,3},{3,2},{4,5},{5,4},{6,7},{7,6},{8,9},{9,8},{10,11... | collective-permute-start | bytes 393224 | tf_op jit(solution)/shard_map/ppermute | solution.py:210
  17.8 1.7 %collective-permute-done.6.refs_7_ = bf16[16,16,256]{2,1,0:T(8,128)(2,1)S(1)} collective-permute-done((bf16[16,16,256]{2,1,0:T(8,128)(2,1)S(1)}, bf16[16,16,256]{2,1,0:T(8,128)(2,1)S(1)}, u32[]{:S(2)}, u32[]{:S(2)}) %collective-permute-start.6) | collective-permute-done | bytes 131104 | tf_op jit(solution)/shard_map/ppermute | solution.py:204
  19.5 0.0 collective-permute-start.8
  19.5 2.4 %collective-permute-done.5.refs_6_ = bf16[16,16,256]{2,1,0:T(8,128)(2,1)S(1)} collective-permute-done((bf16[16,16,256]{2,1,0:T(8,128)(2,1)S(1)}, bf16[16,16,256]{2,1,0:T(8,128)(2,1)S(1)}, u32[]{:S(2)}, u32[]{:S(2)}) %collective-permute-start.5) | collective-permute-done | bytes 131104 | tf_op jit(solution)/shard_map/ppermute | solution.py:204
  21.9 0.0 collective-permute-start.14
  21.9 0.0 collective-permute-done.4.refs_5_
  21.9 0.5 %collective-permute-start.13 = (bf16[16,16,256]{2,1,0:T(8,128)(2,1)S(1)}, bf16[16,16,256]{2,1,0:T(8,128)(2,1)S(1)}, u32[]{:S(2)}, u32[]{:S(2)}) collective-permute-start(bf16[16,16,256]{2,1,0:T(8,128)(2,1)S(1)} %collective-permute-done.5.refs_6_), channel_id=1, source_target_pairs={{0,1},{1,0},{2,3},{3,2},{4,5},{5,4},{6,7},{7,6},{8,9},{9,8},{10,11... | collective-permute-start | bytes 393224 | tf_op jit(solution)/shard_map/ppermute | solution.py:210
  22.4 0.0 collective-permute-done.10.refs_11_
  22.4 0.1 collective-permute-start.12
  22.5 0.0 collective-permute-done.9.refs_10_
  22.5 0.0 collective-permute-done.8.refs_9_
  22.5 0.8 %collective-permute-done.14.refs_15_ = bf16[16,16,256]{2,1,0:T(8,128)(2,1)S(1)} collective-permute-done((bf16[16,16,256]{2,1,0:T(8,128)(2,1)S(1)}, bf16[16,16,256]{2,1,0:T(8,128)(2,1)S(1)}, u32[]{:S(2)}, u32[]{:S(2)}) %collective-permute-start.14) | collective-permute-done | bytes 131104 | tf_op jit(solution)/shard_map/ppermute | solution.py:210
  23.2 0.2 collective-permute-done.13.refs_14_
  23.4 0.3 %collective-permute-done.12.refs_13_ = bf16[16,16,256]{2,1,0:T(8,128)(2,1)S(1)} collective-permute-done((bf16[16,16,256]{2,1,0:T(8,128)(2,1)S(1)}, bf16[16,16,256]{2,1,0:T(8,128)(2,1)S(1)}, u32[]{:S(2)}, u32[]{:S(2)}) %collective-permute-start.12) | collective-permute-done | bytes 131104 | tf_op jit(solution)/shard_map/ppermute | solution.py:210
  23.8 4.7 %shard_map.56 = bf16[64,128,256]{2,1,0:T(8,128)(2,1)} custom-call(bf16[16,16,256]{2,1,0:T(8,128)(2,1)S(1)} %shard_map.55.refs_0_, bf16[16,16,256]{2,1,0:T(8,128)(2,1)S(1)} %collective-permute-done.refs_1_, bf16[16,16,256]{2,1,0:T(8,128)(2,1)S(1)} %collective-permute-done.1.refs_2_, bf16[16,16,256]{2,1,0:T(8,128)(2,1)S(1)} %collective-permute-done.2.refs_3_, ...), custom_call_target="tpu_custom_call" | custom-call | tf_op jit(solution)/shard_map/pallas_call | solution.py:177
Async XLA Ops:
  0.9 10.5 %collective-permute-start.3 = (bf16[16,16,256]{2,1,0:T(8,128)(2,1)S(1)}, bf16[16,16,256]{2,1,0:T(8,128)(2,1)S(1)}, u32[]{:S(2)}, u32[]{:S(2)}) collective-permute-start(bf16[16,16,256]{2,1,0:T(8,128)(2,1)S(1)} %shard_map.55.refs_0_), channel_id=1, source_target_pairs={{0,8},{2,10},{4,12},{6,14},{8,0},{10,2},{12,4},{14,6},{1,9},{3,11}... | collective-permute-start | bytes 393224 | tf_op jit(solution)/shard_map/ppermute | solution.py:204
  5.0 6.4 %collective-permute-start.7 = (bf16[16,16,256]{2,1,0:T(8,128)(2,1)S(1)}, bf16[16,16,256]{2,1,0:T(8,128)(2,1)S(1)}, u32[]{:S(2)}, u32[]{:S(2)}) collective-permute-start(bf16[16,16,256]{2,1,0:T(8,128)(2,1)S(1)} %shard_map.55.refs_0_), channel_id=1, source_target_pairs={{0,1},{1,0},{2,3},{3,2},{4,5},{5,4},{6,7},{7,6},{8,9},{9,8},{10,11... | collective-permute-start | bytes 393224 | tf_op jit(solution)/shard_map/ppermute | solution.py:210
  5.0 8.9 %collective-permute-start.2 = (bf16[16,16,256]{2,1,0:T(8,128)(2,1)S(1)}, bf16[16,16,256]{2,1,0:T(8,128)(2,1)S(1)}, u32[]{:S(2)}, u32[]{:S(2)}) collective-permute-start(bf16[16,16,256]{2,1,0:T(8,128)(2,1)S(1)} %shard_map.55.refs_0_), channel_id=1, source_target_pairs={{0,6},{2,4},{4,2},{6,0},{8,14},{10,12},{12,10},{14,8},{1,7},{3,5},... | collective-permute-start | bytes 393224 | tf_op jit(solution)/shard_map/ppermute | solution.py:204
  7.5 9.0 %collective-permute-start.1 = (bf16[16,16,256]{2,1,0:T(8,128)(2,1)S(1)}, bf16[16,16,256]{2,1,0:T(8,128)(2,1)S(1)}, u32[]{:S(2)}, u32[]{:S(2)}) collective-permute-start(bf16[16,16,256]{2,1,0:T(8,128)(2,1)S(1)} %shard_map.55.refs_0_), channel_id=1, source_target_pairs={{0,4},{2,6},{4,0},{6,2},{8,12},{10,14},{12,8},{14,10},{1,5},{3,7},... | collective-permute-start | bytes 393224 | tf_op jit(solution)/shard_map/ppermute | solution.py:204
  8.0 9.3 %collective-permute-start = (bf16[16,16,256]{2,1,0:T(8,128)(2,1)S(1)}, bf16[16,16,256]{2,1,0:T(8,128)(2,1)S(1)}, u32[]{:S(2)}, u32[]{:S(2)}) collective-permute-start(bf16[16,16,256]{2,1,0:T(8,128)(2,1)S(1)} %shard_map.55.refs_0_), channel_id=1, source_target_pairs={{0,2},{2,0},{4,6},{6,4},{8,10},{10,8},{12,14},{14,12},{1,3},{3,1},... | collective-permute-start | bytes 393224 | tf_op jit(solution)/shard_map/ppermute | solution.py:204
  11.4 5.9 %collective-permute-start.11 = (bf16[16,16,256]{2,1,0:T(8,128)(2,1)S(1)}, bf16[16,16,256]{2,1,0:T(8,128)(2,1)S(1)}, u32[]{:S(2)}, u32[]{:S(2)}) collective-permute-start(bf16[16,16,256]{2,1,0:T(8,128)(2,1)S(1)} %collective-permute-done.3.refs_4_), channel_id=1, source_target_pairs={{0,1},{1,0},{2,3},{3,2},{4,5},{5,4},{6,7},{7,6},{8,9},{9,8},{10,11... | collective-permute-start | bytes 393224 | tf_op jit(solution)/shard_map/ppermute | solution.py:210
  11.4 8.1 %collective-permute-start.6 = (bf16[16,16,256]{2,1,0:T(8,128)(2,1)S(1)}, bf16[16,16,256]{2,1,0:T(8,128)(2,1)S(1)}, u32[]{:S(2)}, u32[]{:S(2)}) collective-permute-start(bf16[16,16,256]{2,1,0:T(8,128)(2,1)S(1)} %collective-permute-done.3.refs_4_), channel_id=1, source_target_pairs={{0,6},{2,4},{4,2},{6,0},{8,14},{10,12},{12,10},{14,8},{1,7},{3,5},... | collective-permute-start | bytes 393224 | tf_op jit(solution)/shard_map/ppermute | solution.py:204
  13.9 8.0 %collective-permute-start.5 = (bf16[16,16,256]{2,1,0:T(8,128)(2,1)S(1)}, bf16[16,16,256]{2,1,0:T(8,128)(2,1)S(1)}, u32[]{:S(2)}, u32[]{:S(2)}) collective-permute-start(bf16[16,16,256]{2,1,0:T(8,128)(2,1)S(1)} %collective-permute-done.3.refs_4_), channel_id=1, source_target_pairs={{0,4},{2,6},{4,0},{6,2},{8,12},{10,14},{12,8},{14,10},{1,5},{3,7},... | collective-permute-start | bytes 393224 | tf_op jit(solution)/shard_map/ppermute | solution.py:204
  16.5 5.4 %collective-permute-start.4 = (bf16[16,16,256]{2,1,0:T(8,128)(2,1)S(1)}, bf16[16,16,256]{2,1,0:T(8,128)(2,1)S(1)}, u32[]{:S(2)}, u32[]{:S(2)}) collective-permute-start(bf16[16,16,256]{2,1,0:T(8,128)(2,1)S(1)} %collective-permute-done.3.refs_4_), channel_id=1, source_target_pairs={{0,2},{2,0},{4,6},{6,4},{8,10},{10,8},{12,14},{14,12},{1,3},{3,1},... | collective-permute-start | bytes 393224 | tf_op jit(solution)/shard_map/ppermute | solution.py:204
  17.3 5.1 %collective-permute-start.10 = (bf16[16,16,256]{2,1,0:T(8,128)(2,1)S(1)}, bf16[16,16,256]{2,1,0:T(8,128)(2,1)S(1)}, u32[]{:S(2)}, u32[]{:S(2)}) collective-permute-start(bf16[16,16,256]{2,1,0:T(8,128)(2,1)S(1)} %collective-permute-done.2.refs_3_), channel_id=1, source_target_pairs={{0,1},{1,0},{2,3},{3,2},{4,5},{5,4},{6,7},{7,6},{8,9},{9,8},{10,11... | collective-permute-start | bytes 393224 | tf_op jit(solution)/shard_map/ppermute | solution.py:210
  17.3 5.2 %collective-permute-start.9 = (bf16[16,16,256]{2,1,0:T(8,128)(2,1)S(1)}, bf16[16,16,256]{2,1,0:T(8,128)(2,1)S(1)}, u32[]{:S(2)}, u32[]{:S(2)}) collective-permute-start(bf16[16,16,256]{2,1,0:T(8,128)(2,1)S(1)} %collective-permute-done.1.refs_2_), channel_id=1, source_target_pairs={{0,1},{1,0},{2,3},{3,2},{4,5},{5,4},{6,7},{7,6},{8,9},{9,8},{10,11... | collective-permute-start | bytes 393224 | tf_op jit(solution)/shard_map/ppermute | solution.py:210
  19.5 3.0 %collective-permute-start.8 = (bf16[16,16,256]{2,1,0:T(8,128)(2,1)S(1)}, bf16[16,16,256]{2,1,0:T(8,128)(2,1)S(1)}, u32[]{:S(2)}, u32[]{:S(2)}) collective-permute-start(bf16[16,16,256]{2,1,0:T(8,128)(2,1)S(1)} %collective-permute-done.refs_1_), channel_id=1, source_target_pairs={{0,1},{1,0},{2,3},{3,2},{4,5},{5,4},{6,7},{7,6},{8,9},{9,8},{10,11... | collective-permute-start | bytes 393224 | tf_op jit(solution)/shard_map/ppermute | solution.py:210
  21.9 1.3 %collective-permute-start.14 = (bf16[16,16,256]{2,1,0:T(8,128)(2,1)S(1)}, bf16[16,16,256]{2,1,0:T(8,128)(2,1)S(1)}, u32[]{:S(2)}, u32[]{:S(2)}) collective-permute-start(bf16[16,16,256]{2,1,0:T(8,128)(2,1)S(1)} %collective-permute-done.6.refs_7_), channel_id=1, source_target_pairs={{0,1},{1,0},{2,3},{3,2},{4,5},{5,4},{6,7},{7,6},{8,9},{9,8},{10,11... | collective-permute-start | bytes 393224 | tf_op jit(solution)/shard_map/ppermute | solution.py:210
  21.9 1.5 %collective-permute-start.13 = (bf16[16,16,256]{2,1,0:T(8,128)(2,1)S(1)}, bf16[16,16,256]{2,1,0:T(8,128)(2,1)S(1)}, u32[]{:S(2)}, u32[]{:S(2)}) collective-permute-start(bf16[16,16,256]{2,1,0:T(8,128)(2,1)S(1)} %collective-permute-done.5.refs_6_), channel_id=1, source_target_pairs={{0,1},{1,0},{2,3},{3,2},{4,5},{5,4},{6,7},{7,6},{8,9},{9,8},{10,11... | collective-permute-start | bytes 393224 | tf_op jit(solution)/shard_map/ppermute | solution.py:210
  22.4 1.3 %collective-permute-start.12 = (bf16[16,16,256]{2,1,0:T(8,128)(2,1)S(1)}, bf16[16,16,256]{2,1,0:T(8,128)(2,1)S(1)}, u32[]{:S(2)}, u32[]{:S(2)}) collective-permute-start(bf16[16,16,256]{2,1,0:T(8,128)(2,1)S(1)} %collective-permute-done.4.refs_5_), channel_id=1, source_target_pairs={{0,1},{1,0},{2,3},{3,2},{4,5},{5,4},{6,7},{7,6},{8,9},{9,8},{10,11... | collective-permute-start | bytes 393224 | tf_op jit(solution)/shard_map/ppermute | solution.py:210

commit v2 on v0

--- a/solution.py
+++ b/solution.py
@@ -1,7 +1,16 @@
+import functools
+
 import jax
 import jax.numpy as jnp
 from jax import lax
+from jax.experimental import pallas as pl
+from jax.experimental.pallas import tpu as pltpu
 from jax.sharding import PartitionSpec as P
+
+CHUNK = 4
+ANY = pl.BlockSpec(memory_space=pl.ANY)
+SMEM = pl.BlockSpec(memory_space=pltpu.SMEM)
+VMEM = pl.BlockSpec(memory_space=pltpu.VMEM)
 
 
 def placing(blocks, row_home, stored, owners, capacity):
@@ -49,7 +58,7 @@
     return (-product).astype(jnp.bfloat16)
 
 
-def body(forward, adjoint, row_home, block_rows, block_cols):
+def tabled(forward, adjoint, row_home, block_rows, block_cols):
     owners = lax.axis_size("blk")
     stored = forward.shape[0]
     slot_count = block_rows.shape[1]
@@ -67,6 +76,127 @@
     return result.reshape(2, slot_count, half_width, width)
 
 
+def load_kernel(a, b, home, rows, cols, out, home_s, rows_s, cols_s, sem):
+    n = a.shape[0]
+    pairs = (
+        (a, out.at[pl.ds(0, n)]),
+        (b, out.at[pl.ds(n, n)]),
+        (home, home_s),
+        (rows, rows_s),
+        (cols, cols_s),
+    )
+    copies = [pltpu.make_async_copy(*pair, sem.at[k]) for k, pair in enumerate(pairs)]
+    for copy in copies:
+        copy.start()
+    for copy in copies:
+        copy.wait()
+
+
+def load(a, b, index):
+    return pl.pallas_call(
+        load_kernel,
+        out_shape=[pltpu.VMEM((2 * a.shape[0],) + a.shape[1:], a.dtype)]
+        + [pltpu.SMEM(v.shape, v.dtype) for v in index],
+        in_specs=[ANY] * 5,
+        out_specs=[VMEM] + [SMEM] * 3,
+        scratch_shapes=[pltpu.SemaphoreType.DMA((5,))],
+        compiler_params=pltpu.CompilerParams(vmem_limit_bytes=1 << 20),
+    )(*(pltpu.with_memory_space_constraint(v, pltpu.HBM) for v in (a, b) + index))
+
+
+def stage(shards, left, right):
+    joined, rhs, _ = shards[0].shape
+    stored, half = joined // 2, left.shape[2]
+    start = pl.multiple_of(lax.axis_index("rhs") * half, half)
+    for n, shard in enumerate(shards):
+        slots = slice(n // 2 * stored, (n // 2 + 1) * stored)
+        part = slice(n % 2 * rhs, (n % 2 + 1) * rhs)
+        right[slots, part] = shard[:stored]
+        left[slots, part] = -shard[stored:, :, pl.ds(start, half)]
+
+
+def products_kernel(stored, *refs):
+    shards, refs = refs[:-8], refs[-8:]
+    home, rows, cols, out, left, right, result, sem = refs
+    stage(shards, left, right)
+    mine = lax.axis_index("blk") * stored
+    strips, per_strip = rows.shape
+    chunks = strips * per_strip // CHUNK
+
+    def out_copy(n):
+        part = pl.ds(n * CHUNK, CHUNK)
+        return pltpu.make_async_copy(result.at[part], out.at[part], sem.at[n])
+
+    def one_strip(strip, carry):
+        for k in range(per_strip):
+            a = left[jnp.bitwise_xor(home[rows[strip, k]], mine)]
+            b = right[jnp.bitwise_xor(home[cols[strip, k]], mine)]
+            product = lax.dot_general(
+                a, b, (((0,), (0,)), ((), ())), preferred_element_type=jnp.float32
+            )
+            result[strip * per_strip + k] = product.astype(jnp.bfloat16)
+            if k % CHUNK == CHUNK - 1:
+                out_copy(strip * (per_strip // CHUNK) + k // CHUNK).start()
+        return carry
+
+    lax.fori_loop(0, strips, one_strip, 0)
+
+    def drain(n, carry):
+        out_copy(n).wait()
+        return carry
+
+    lax.fori_loop(0, chunks, drain, 0)
+
+
+def products(shards, index):
+    joined, rhs, width = shards[0].shape
+    stored, half = joined // 2, width // 2
+    slots = len(shards) // 2 * stored
+    entries = index[1].size
+    out = jax.ShapeDtypeStruct((entries, half, width), jnp.bfloat16)
+    return pl.pallas_call(
+        functools.partial(products_kernel, stored),
+        out_shape=out,
+        in_specs=[VMEM] * len(shards) + [SMEM] * 3,
+        out_specs=ANY,
+        scratch_shapes=[
+            pltpu.VMEM((slots, 2 * rhs, half), jnp.bfloat16),
+            pltpu.VMEM((slots, 2 * rhs, width), jnp.bfloat16),
+            pltpu.VMEM(out.shape, out.dtype),
+            pltpu.SemaphoreType.DMA((entries // CHUNK,)),
+        ],
+        compiler_params=pltpu.CompilerParams(vmem_limit_bytes=16 << 20),
+    )(*shards, *index)
+
+
+PLAN = ((4, 4), (3, 3), (2, 2), (1, 1), (7, 3), (6, 2), (5, 1))
+
+
+def gathered(forward, adjoint, row_home, block_rows, block_cols):
+    owners = lax.axis_size("blk")
+
+    def across(value, mask):
+        return lax.ppermute(value, "blk", [(i, i ^ mask) for i in range(owners)])
+
+    own, *index = load(forward, adjoint, (row_home, block_rows, block_cols))
+    held = {0: own}
+    for mask, via in PLAN:
+        held[mask] = across(held[mask ^ via], via)
+    shards = []
+    for j in range(owners):
+        shards += [held[j], lax.ppermute(held[j], "rhs", [(0, 1), (1, 0)])]
+    result = products(shards, index)
+    return result.reshape(2, block_rows.shape[1], *result.shape[1:])
+
+
+def body(forward, adjoint, row_home, block_rows, block_cols):
+    owners, stored = lax.axis_size("blk"), forward.shape[0]
+    few = owners * stored <= 2 * block_rows.shape[1]
+    if few and owners == 8 and stored & (stored - 1) == 0 and block_rows.shape[1] % CHUNK == 0:
+        return gathered(forward, adjoint, row_home, block_rows, block_cols)
+    return tabled(forward, adjoint, row_home, block_rows, block_cols)
+
+
 def solution(mesh):
     placed = (
         P(("groups", "blk"), "rhs", None),

time: 89.2 us -> 26 us (0.29)
  waiting for transfers between devices: 39.8 us -> 9.8 us
  between operations: 13.6 us -> 0.03 us
  local copies, waits for them, and re-layouts: 8.32 us -> 0 us
  starting transfers between devices: 17.8 us -> 12.5 us
  matrix products: 4.7 us -> 0 us
  other arithmetic: 4.47 us -> 0 us
  Pallas kernels: 0 us -> 3.57 us
    all_to_all x4 -> x0, waiting for transfers between devices: 30 us -> none  [the longest x1 11.5 us: fetch(): lax.all_to_all(right, 'blk', split_axis=0, concat_axis=0, tiled=True)]
    all_to_all x4 -> x0, starting transfers between devices: 17.7 us -> none  [the longest x1 7.25 us: fetch(): lax.all_to_all(row_table, 'blk', split_axis=0, concat_axis=0, tiled=True)]
    ppermute x0 -> x15, starting transfers between devices: none -> 12.5 us  [the longest x7 11.3 us: across(): return lax.ppermute(value, 'blk', [(i, i ^ mask) for i in range(owners)])]
    all_gather x2 -> x0, waiting for transfers between devices: 9.84 us -> none  [the longest x1 9.82 us: finish(): lax.all_gather(right, 'rhs', axis=1, tiled=True)]
    ppermute x0 -> x15, waiting for transfers between devices: none -> 9.8 us  [the longest x7 8.59 us: across(): return lax.ppermute(value, 'blk', [(i, i ^ mask) for i in range(owners)])]
    gather x6 -> x0, local copies, waits for them, and re-layouts: 5.23 us -> none  [the longest x2 2.85 us: placing(): slot_of = jnp.take(row_home, blocks)]
    dot_general x1 -> x0, matrix products: 4.7 us -> none  [finish(): jnp.einsum('kra,krb->kab', left, right, preferred_element_type=jnp.float32)]
    select_n x14 -> x0, other arithmetic: 3.83 us -> none  [the longest x4 1.89 us: select(): return jnp.take(flat, place, axis=0)]
  transfers between devices with their start and end apart: 6 -> 15, of which waited for: 5 -> 10; matrix products, arithmetic and copies ran while one was open for 10% -> 0% of each run, Pallas kernels for 0% -> 0%
where the time goes in v2:
time: 26 us; the launch traced here: 25.9 us
  starting transfers between devices  12.5 us (48%)
  waiting for transfers between devices  9.8 us (38%)
  Pallas kernels  3.57 us (14%)
    ppermute x7, starting transfers between devices, across(): return lax.ppermute(value, 'blk', [(i, i ^ mask) for i in range(owners)])  11.3 us
    ppermute x7, waiting for transfers between devices, across(): return lax.ppermute(value, 'blk', [(i, i ^ mask) for i in range(owners)])  8.59 us
    pallas_call x1, Pallas kernels, products(): pl.pallas_call(functools.partial(products_kernel, stored), out_shape=out,...  2.64 us
    ppermute x8, waiting for transfers between devices, gathered(): shards += [held[j], lax.ppermute(held[j], 'rhs', [(0, 1), (1, 0)])]  1.22 us
    ppermute x8, starting transfers between devices, gathered(): shards += [held[j], lax.ppermute(held[j], 'rhs', [(0, 1), (1, 0)])]  1.17 us
    pallas_call x1, Pallas kernels, load(): pl.pallas_call(load_kernel, out_shape=[pltpu.VMEM((2 * a.shape[0],) + a.s...  0.94 us
  transfers between devices with their start and end apart: 15, of which 10 were waited for; matrix products, arithmetic and copies ran while one was open for 0% of the time, Pallas kernels for 0%

profile of v2, /device:TPU:0, one launch (start us, length us, event | category | flops | bytes accessed | tf_op | source)
XLA Modules:
  0.0 25.9 jit_solution(16170986358715449186)
XLA Ops:
  0.0 0.9 %shard_map.55 = (bf16[16,16,256]{2,1,0:T(8,128)(2,1)S(1)}, s32[64]{0:T(128)S(4)}, s32[2,32]{1,0:T(2,128)S(4)}, s32[2,32]{1,0:T(2,128)S(4)}) custom-call(bf16[8,16,256]{2,1,0:T(8,128)(2,1)} %a.1, bf16[8,16,256]{2,1,0:T(8,128)(2,1)} %b.1, s32[64]{0:T(128)} %home.1, s32[2,32]{1,0:T(2,128)} %rows.1, s32[2,32]{1,0:T(2,128)} %cols.1), custom_call_target="tpu_custom_call" | custom-call | tf_op jit(solution)/shard_map/pallas_call | solution.py:96
  0.9 4.1 %collective-permute-start.7 = (bf16[16,16,256]{2,1,0:T(8,128)(2,1)S(1)}, bf16[16,16,256]{2,1,0:T(8,128)(2,1)S(1)}, u32[]{:S(2)}, u32[]{:S(2)}) collective-permute-start(bf16[16,16,256]{2,1,0:T(8,128)(2,1)S(1)} %get-tuple-element.9.refs_0_), channel_id=1, source_target_pairs={{0,8},{2,10},{4,12},{6,14},{8,0},{10,2},{12,4},{14,6},{1,9},{3,11}... | collective-permute-start | bytes 393224 | tf_op jit(solution)/shard_map/ppermute | solution.py:179
  5.0 2.5 %collective-permute-start.5 = (bf16[16,16,256]{2,1,0:T(8,128)(2,1)S(1)}, bf16[16,16,256]{2,1,0:T(8,128)(2,1)S(1)}, u32[]{:S(2)}, u32[]{:S(2)}) collective-permute-start(bf16[16,16,256]{2,1,0:T(8,128)(2,1)S(1)} %get-tuple-element.9.refs_0_), channel_id=1, source_target_pairs={{0,6},{2,4},{4,2},{6,0},{8,14},{10,12},{12,10},{14,8},{1,7},{3,5},... | collective-permute-start | bytes 393224 | tf_op jit(solution)/shard_map/ppermute | solution.py:179
  7.6 0.4 %collective-permute-start.3 = (bf16[16,16,256]{2,1,0:T(8,128)(2,1)S(1)}, bf16[16,16,256]{2,1,0:T(8,128)(2,1)S(1)}, u32[]{:S(2)}, u32[]{:S(2)}) collective-permute-start(bf16[16,16,256]{2,1,0:T(8,128)(2,1)S(1)} %get-tuple-element.9.refs_0_), channel_id=1, source_target_pairs={{0,4},{2,6},{4,0},{6,2},{8,12},{10,14},{12,8},{14,10},{1,5},{3,7},... | collective-permute-start | bytes 393224 | tf_op jit(solution)/shard_map/ppermute | solution.py:179
  8.0 0.5 %collective-permute-start.1 = (bf16[16,16,256]{2,1,0:T(8,128)(2,1)S(1)}, bf16[16,16,256]{2,1,0:T(8,128)(2,1)S(1)}, u32[]{:S(2)}, u32[]{:S(2)}) collective-permute-start(bf16[16,16,256]{2,1,0:T(8,128)(2,1)S(1)} %get-tuple-element.9.refs_0_), channel_id=1, source_target_pairs={{0,2},{2,0},{4,6},{6,4},{8,10},{10,8},{12,14},{14,12},{1,3},{3,1},... | collective-permute-start | bytes 393224 | tf_op jit(solution)/shard_map/ppermute | solution.py:179
  8.5 0.0 collective-permute-start
  8.5 2.9 %collective-permute-done.7.refs_8_ = bf16[16,16,256]{2,1,0:T(8,128)(2,1)S(1)} collective-permute-done((bf16[16,16,256]{2,1,0:T(8,128)(2,1)S(1)}, bf16[16,16,256]{2,1,0:T(8,128)(2,1)S(1)}, u32[]{:S(2)}, u32[]{:S(2)}) %collective-permute-start.7) | collective-permute-done | bytes 131104 | tf_op jit(solution)/shard_map/ppermute | solution.py:179
  11.5 1.6 %collective-permute-start.13 = (bf16[16,16,256]{2,1,0:T(8,128)(2,1)S(1)}, bf16[16,16,256]{2,1,0:T(8,128)(2,1)S(1)}, u32[]{:S(2)}, u32[]{:S(2)}) collective-permute-start(bf16[16,16,256]{2,1,0:T(8,128)(2,1)S(1)} %collective-permute-done.7.refs_8_), channel_id=1, source_target_pairs={{0,6},{2,4},{4,2},{6,0},{8,14},{10,12},{12,10},{14,8},{1,7},{3,5},... | collective-permute-start | bytes 393224 | tf_op jit(solution)/shard_map/ppermute | solution.py:179
  13.0 1.0 %collective-permute-done.5.refs_6_ = bf16[16,16,256]{2,1,0:T(8,128)(2,1)S(1)} collective-permute-done((bf16[16,16,256]{2,1,0:T(8,128)(2,1)S(1)}, bf16[16,16,256]{2,1,0:T(8,128)(2,1)S(1)}, u32[]{:S(2)}, u32[]{:S(2)}) %collective-permute-start.5) | collective-permute-done | bytes 131104 | tf_op jit(solution)/shard_map/ppermute | solution.py:179
  14.1 1.1 %collective-permute-start.11 = (bf16[16,16,256]{2,1,0:T(8,128)(2,1)S(1)}, bf16[16,16,256]{2,1,0:T(8,128)(2,1)S(1)}, u32[]{:S(2)}, u32[]{:S(2)}) collective-permute-start(bf16[16,16,256]{2,1,0:T(8,128)(2,1)S(1)} %collective-permute-done.7.refs_8_), channel_id=1, source_target_pairs={{0,4},{2,6},{4,0},{6,2},{8,12},{10,14},{12,8},{14,10},{1,5},{3,7},... | collective-permute-start | bytes 393224 | tf_op jit(solution)/shard_map/ppermute | solution.py:179
  15.2 1.2 %collective-permute-done.3.refs_4_ = bf16[16,16,256]{2,1,0:T(8,128)(2,1)S(1)} collective-permute-done((bf16[16,16,256]{2,1,0:T(8,128)(2,1)S(1)}, bf16[16,16,256]{2,1,0:T(8,128)(2,1)S(1)}, u32[]{:S(2)}, u32[]{:S(2)}) %collective-permute-start.3) | collective-permute-done | bytes 131104 | tf_op jit(solution)/shard_map/ppermute | solution.py:179
  16.4 1.0 %collective-permute-start.9 = (bf16[16,16,256]{2,1,0:T(8,128)(2,1)S(1)}, bf16[16,16,256]{2,1,0:T(8,128)(2,1)S(1)}, u32[]{:S(2)}, u32[]{:S(2)}) collective-permute-start(bf16[16,16,256]{2,1,0:T(8,128)(2,1)S(1)} %collective-permute-done.7.refs_8_), channel_id=1, source_target_pairs={{0,2},{2,0},{4,6},{6,4},{8,10},{10,8},{12,14},{14,12},{1,3},{3,1},... | collective-permute-start | bytes 393224 | tf_op jit(solution)/shard_map/ppermute | solution.py:179
  17.4 0.0 collective-permute-done.1.refs_2_
  17.4 0.0 collective-permute-start.8
  17.4 0.0 collective-permute-done.refs_1_
  17.5 0.5 %collective-permute-start.6 = (bf16[16,16,256]{2,1,0:T(8,128)(2,1)S(1)}, bf16[16,16,256]{2,1,0:T(8,128)(2,1)S(1)}, u32[]{:S(2)}, u32[]{:S(2)}) collective-permute-start(bf16[16,16,256]{2,1,0:T(8,128)(2,1)S(1)} %collective-permute-done.5.refs_6_), channel_id=1, source_target_pairs={{0,1},{1,0},{2,3},{3,2},{4,5},{5,4},{6,7},{7,6},{8,9},{9,8},{10,11... | collective-permute-start | bytes 393224 | tf_op jit(solution)/shard_map/ppermute | solution.py:187
  18.0 1.8 %collective-permute-done.13.refs_14_ = bf16[16,16,256]{2,1,0:T(8,128)(2,1)S(1)} collective-permute-done((bf16[16,16,256]{2,1,0:T(8,128)(2,1)S(1)}, bf16[16,16,256]{2,1,0:T(8,128)(2,1)S(1)}, u32[]{:S(2)}, u32[]{:S(2)}) %collective-permute-start.13) | collective-permute-done | bytes 131104 | tf_op jit(solution)/shard_map/ppermute | solution.py:179
  19.7 0.0 collective-permute-start.4
  19.7 1.3 %collective-permute-done.11.refs_12_ = bf16[16,16,256]{2,1,0:T(8,128)(2,1)S(1)} collective-permute-done((bf16[16,16,256]{2,1,0:T(8,128)(2,1)S(1)}, bf16[16,16,256]{2,1,0:T(8,128)(2,1)S(1)}, u32[]{:S(2)}, u32[]{:S(2)}) %collective-permute-start.11) | collective-permute-done | bytes 131104 | tf_op jit(solution)/shard_map/ppermute | solution.py:179
  21.0 0.0 collective-permute-start.2
  21.0 0.4 %collective-permute-done.9.refs_10_ = bf16[16,16,256]{2,1,0:T(8,128)(2,1)S(1)} collective-permute-done((bf16[16,16,256]{2,1,0:T(8,128)(2,1)S(1)}, bf16[16,16,256]{2,1,0:T(8,128)(2,1)S(1)}, u32[]{:S(2)}, u32[]{:S(2)}) %collective-permute-start.9) | collective-permute-done | bytes 131104 | tf_op jit(solution)/shard_map/ppermute | solution.py:179
  21.4 0.1 collective-permute-start.14
  21.5 0.0 collective-permute-done.8.refs_9_
  21.5 0.4 %collective-permute-start.12 = (bf16[16,16,256]{2,1,0:T(8,128)(2,1)S(1)}, bf16[16,16,256]{2,1,0:T(8,128)(2,1)S(1)}, u32[]{:S(2)}, u32[]{:S(2)}) collective-permute-start(bf16[16,16,256]{2,1,0:T(8,128)(2,1)S(1)} %collective-permute-done.11.refs_12_), channel_id=1, source_target_pairs={{0,1},{1,0},{2,3},{3,2},{4,5},{5,4},{6,7},{7,6},{8,9},{9,8},{10,11... | collective-permute-start | bytes 393224 | tf_op jit(solution)/shard_map/ppermute | solution.py:187
  21.9 0.0 collective-permute-done.6.refs_7_
  21.9 0.1 collective-permute-start.10
  22.0 0.0 collective-permute-done.4.refs_5_
  22.0 0.3 %collective-permute-done.2.refs_3_ = bf16[16,16,256]{2,1,0:T(8,128)(2,1)S(1)} collective-permute-done((bf16[16,16,256]{2,1,0:T(8,128)(2,1)S(1)}, bf16[16,16,256]{2,1,0:T(8,128)(2,1)S(1)}, u32[]{:S(2)}, u32[]{:S(2)}) %collective-permute-start.2) | collective-permute-done | bytes 131104 | tf_op jit(solution)/shard_map/ppermute | solution.py:187
  22.4 0.4 %collective-permute-done.14.refs_15_ = bf16[16,16,256]{2,1,0:T(8,128)(2,1)S(1)} collective-permute-done((bf16[16,16,256]{2,1,0:T(8,128)(2,1)S(1)}, bf16[16,16,256]{2,1,0:T(8,128)(2,1)S(1)}, u32[]{:S(2)}, u32[]{:S(2)}) %collective-permute-start.14) | collective-permute-done | bytes 131104 | tf_op jit(solution)/shard_map/ppermute | solution.py:187
  22.7 0.2 collective-permute-done.12.refs_13_
  22.9 0.3 %collective-permute-done.10.refs_11_ = bf16[16,16,256]{2,1,0:T(8,128)(2,1)S(1)} collective-permute-done((bf16[16,16,256]{2,1,0:T(8,128)(2,1)S(1)}, bf16[16,16,256]{2,1,0:T(8,128)(2,1)S(1)}, u32[]{:S(2)}, u32[]{:S(2)}) %collective-permute-start.10) | collective-permute-done | bytes 131104 | tf_op jit(solution)/shard_map/ppermute | solution.py:187
  23.3 2.6 %shard_map.56 = bf16[64,128,256]{2,1,0:T(8,128)(2,1)} custom-call(bf16[16,16,256]{2,1,0:T(8,128)(2,1)S(1)} %get-tuple-element.9.refs_0_, bf16[16,16,256]{2,1,0:T(8,128)(2,1)S(1)} %collective-permute-done.refs_1_, bf16[16,16,256]{2,1,0:T(8,128)(2,1)S(1)} %collective-permute-done.1.refs_2_, bf16[16,16,256]{2,1,0:T(8,128)(2,1)S(1)} %collective-permute-done.2.refs_3_, ...), custom_call_target="tpu_custom_call" | custom-call | tf_op jit(solution)/shard_map/pallas_call | solution.py:157
Async XLA Ops:
  0.9 10.5 %collective-permute-start.7 = (bf16[16,16,256]{2,1,0:T(8,128)(2,1)S(1)}, bf16[16,16,256]{2,1,0:T(8,128)(2,1)S(1)}, u32[]{:S(2)}, u32[]{:S(2)}) collective-permute-start(bf16[16,16,256]{2,1,0:T(8,128)(2,1)S(1)} %get-tuple-element.9.refs_0_), channel_id=1, source_target_pairs={{0,8},{2,10},{4,12},{6,14},{8,0},{10,2},{12,4},{14,6},{1,9},{3,11}... | collective-permute-start | bytes 393224 | tf_op jit(solution)/shard_map/ppermute | solution.py:179
  5.0 9.0 %collective-permute-start.5 = (bf16[16,16,256]{2,1,0:T(8,128)(2,1)S(1)}, bf16[16,16,256]{2,1,0:T(8,128)(2,1)S(1)}, u32[]{:S(2)}, u32[]{:S(2)}) collective-permute-start(bf16[16,16,256]{2,1,0:T(8,128)(2,1)S(1)} %get-tuple-element.9.refs_0_), channel_id=1, source_target_pairs={{0,6},{2,4},{4,2},{6,0},{8,14},{10,12},{12,10},{14,8},{1,7},{3,5},... | collective-permute-start | bytes 393224 | tf_op jit(solution)/shard_map/ppermute | solution.py:179
  7.6 8.9 %collective-permute-start.3 = (bf16[16,16,256]{2,1,0:T(8,128)(2,1)S(1)}, bf16[16,16,256]{2,1,0:T(8,128)(2,1)S(1)}, u32[]{:S(2)}, u32[]{:S(2)}) collective-permute-start(bf16[16,16,256]{2,1,0:T(8,128)(2,1)S(1)} %get-tuple-element.9.refs_0_), channel_id=1, source_target_pairs={{0,4},{2,6},{4,0},{6,2},{8,12},{10,14},{12,8},{14,10},{1,5},{3,7},... | collective-permute-start | bytes 393224 | tf_op jit(solution)/shard_map/ppermute | solution.py:179
  8.0 9.4 %collective-permute-start.1 = (bf16[16,16,256]{2,1,0:T(8,128)(2,1)S(1)}, bf16[16,16,256]{2,1,0:T(8,128)(2,1)S(1)}, u32[]{:S(2)}, u32[]{:S(2)}) collective-permute-start(bf16[16,16,256]{2,1,0:T(8,128)(2,1)S(1)} %get-tuple-element.9.refs_0_), channel_id=1, source_target_pairs={{0,2},{2,0},{4,6},{6,4},{8,10},{10,8},{12,14},{14,12},{1,3},{3,1},... | collective-permute-start | bytes 393224 | tf_op jit(solution)/shard_map/ppermute | solution.py:179
  8.5 8.9 %collective-permute-start = (bf16[16,16,256]{2,1,0:T(8,128)(2,1)S(1)}, bf16[16,16,256]{2,1,0:T(8,128)(2,1)S(1)}, u32[]{:S(2)}, u32[]{:S(2)}) collective-permute-start(bf16[16,16,256]{2,1,0:T(8,128)(2,1)S(1)} %get-tuple-element.9.refs_0_), channel_id=1, source_target_pairs={{0,1},{1,0},{2,3},{3,2},{4,5},{5,4},{6,7},{7,6},{8,9},{9,8},{10,11... | collective-permute-start | bytes 393224 | tf_op jit(solution)/shard_map/ppermute | solution.py:187
  11.5 8.3 %collective-permute-start.13 = (bf16[16,16,256]{2,1,0:T(8,128)(2,1)S(1)}, bf16[16,16,256]{2,1,0:T(8,128)(2,1)S(1)}, u32[]{:S(2)}, u32[]{:S(2)}) collective-permute-start(bf16[16,16,256]{2,1,0:T(8,128)(2,1)S(1)} %collective-permute-done.7.refs_8_), channel_id=1, source_target_pairs={{0,6},{2,4},{4,2},{6,0},{8,14},{10,12},{12,10},{14,8},{1,7},{3,5},... | collective-permute-start | bytes 393224 | tf_op jit(solution)/shard_map/ppermute | solution.py:179
  14.1 6.9 %collective-permute-start.11 = (bf16[16,16,256]{2,1,0:T(8,128)(2,1)S(1)}, bf16[16,16,256]{2,1,0:T(8,128)(2,1)S(1)}, u32[]{:S(2)}, u32[]{:S(2)}) collective-permute-start(bf16[16,16,256]{2,1,0:T(8,128)(2,1)S(1)} %collective-permute-done.7.refs_8_), channel_id=1, source_target_pairs={{0,4},{2,6},{4,0},{6,2},{8,12},{10,14},{12,8},{14,10},{1,5},{3,7},... | collective-permute-start | bytes 393224 | tf_op jit(solution)/shard_map/ppermute | solution.py:179
  16.4 5.0 %collective-permute-start.9 = (bf16[16,16,256]{2,1,0:T(8,128)(2,1)S(1)}, bf16[16,16,256]{2,1,0:T(8,128)(2,1)S(1)}, u32[]{:S(2)}, u32[]{:S(2)}) collective-permute-start(bf16[16,16,256]{2,1,0:T(8,128)(2,1)S(1)} %collective-permute-done.7.refs_8_), channel_id=1, source_target_pairs={{0,2},{2,0},{4,6},{6,4},{8,10},{10,8},{12,14},{14,12},{1,3},{3,1},... | collective-permute-start | bytes 393224 | tf_op jit(solution)/shard_map/ppermute | solution.py:179
  17.4 4.1 %collective-permute-start.8 = (bf16[16,16,256]{2,1,0:T(8,128)(2,1)S(1)}, bf16[16,16,256]{2,1,0:T(8,128)(2,1)S(1)}, u32[]{:S(2)}, u32[]{:S(2)}) collective-permute-start(bf16[16,16,256]{2,1,0:T(8,128)(2,1)S(1)} %collective-permute-done.7.refs_8_), channel_id=1, source_target_pairs={{0,1},{1,0},{2,3},{3,2},{4,5},{5,4},{6,7},{7,6},{8,9},{9,8},{10,11... | collective-permute-start | bytes 393224 | tf_op jit(solution)/shard_map/ppermute | solution.py:187
  17.5 4.4 %collective-permute-start.6 = (bf16[16,16,256]{2,1,0:T(8,128)(2,1)S(1)}, bf16[16,16,256]{2,1,0:T(8,128)(2,1)S(1)}, u32[]{:S(2)}, u32[]{:S(2)}) collective-permute-start(bf16[16,16,256]{2,1,0:T(8,128)(2,1)S(1)} %collective-permute-done.5.refs_6_), channel_id=1, source_target_pairs={{0,1},{1,0},{2,3},{3,2},{4,5},{5,4},{6,7},{7,6},{8,9},{9,8},{10,11... | collective-permute-start | bytes 393224 | tf_op jit(solution)/shard_map/ppermute | solution.py:187
  19.7 2.3 %collective-permute-start.4 = (bf16[16,16,256]{2,1,0:T(8,128)(2,1)S(1)}, bf16[16,16,256]{2,1,0:T(8,128)(2,1)S(1)}, u32[]{:S(2)}, u32[]{:S(2)}) collective-permute-start(bf16[16,16,256]{2,1,0:T(8,128)(2,1)S(1)} %collective-permute-done.3.refs_4_), channel_id=1, source_target_pairs={{0,1},{1,0},{2,3},{3,2},{4,5},{5,4},{6,7},{7,6},{8,9},{9,8},{10,11... | collective-permute-start | bytes 393224 | tf_op jit(solution)/shard_map/ppermute | solution.py:187
  21.0 1.3 %collective-permute-start.2 = (bf16[16,16,256]{2,1,0:T(8,128)(2,1)S(1)}, bf16[16,16,256]{2,1,0:T(8,128)(2,1)S(1)}, u32[]{:S(2)}, u32[]{:S(2)}) collective-permute-start(bf16[16,16,256]{2,1,0:T(8,128)(2,1)S(1)} %collective-permute-done.1.refs_2_), channel_id=1, source_target_pairs={{0,1},{1,0},{2,3},{3,2},{4,5},{5,4},{6,7},{7,6},{8,9},{9,8},{10,11... | collective-permute-start | bytes 393224 | tf_op jit(solution)/shard_map/ppermute | solution.py:187
  21.4 1.3 %collective-permute-start.14 = (bf16[16,16,256]{2,1,0:T(8,128)(2,1)S(1)}, bf16[16,16,256]{2,1,0:T(8,128)(2,1)S(1)}, u32[]{:S(2)}, u32[]{:S(2)}) collective-permute-start(bf16[16,16,256]{2,1,0:T(8,128)(2,1)S(1)} %collective-permute-done.13.refs_14_), channel_id=1, source_target_pairs={{0,1},{1,0},{2,3},{3,2},{4,5},{5,4},{6,7},{7,6},{8,9},{9,8},{10,11... | collective-permute-start | bytes 393224 | tf_op jit(solution)/shard_map/ppermute | solution.py:187
  21.5 1.4 %collective-permute-start.12 = (bf16[16,16,256]{2,1,0:T(8,128)(2,1)S(1)}, bf16[16,16,256]{2,1,0:T(8,128)(2,1)S(1)}, u32[]{:S(2)}, u32[]{:S(2)}) collective-permute-start(bf16[16,16,256]{2,1,0:T(8,128)(2,1)S(1)} %collective-permute-done.11.refs_12_), channel_id=1, source_target_pairs={{0,1},{1,0},{2,3},{3,2},{4,5},{5,4},{6,7},{7,6},{8,9},{9,8},{10,11... | collective-permute-start | bytes 393224 | tf_op jit(solution)/shard_map/ppermute | solution.py:187
  21.9 1.3 %collective-permute-start.10 = (bf16[16,16,256]{2,1,0:T(8,128)(2,1)S(1)}, bf16[16,16,256]{2,1,0:T(8,128)(2,1)S(1)}, u32[]{:S(2)}, u32[]{:S(2)}) collective-permute-start(bf16[16,16,256]{2,1,0:T(8,128)(2,1)S(1)} %collective-permute-done.9.refs_10_), channel_id=1, source_target_pairs={{0,1},{1,0},{2,3},{3,2},{4,5},{5,4},{6,7},{7,6},{8,9},{9,8},{10,11... | collective-permute-start | bytes 393224 | tf_op jit(solution)/shard_map/ppermute | solution.py:187

commit v3 on v2

--- a/solution.py
+++ b/solution.py
@@ -169,7 +169,7 @@
     )(*shards, *index)
 
 
-PLAN = ((4, 4), (3, 3), (2, 2), (1, 1), (7, 3), (6, 2), (5, 1))
+PLAN = ((6, 6), (2, 2), (1, 1), (3, 2), (7, 1), (4, 2), (5, 1))
 
 
 def gathered(forward, adjoint, row_home, block_rows, block_cols):

time: 26 us -> 24.6 us (0.946)
  waiting for transfers between devices: 9.8 us -> 7.37 us
  starting transfers between devices: 12.5 us -> 13.4 us
    ppermute x7, waiting for transfers between devices: 8.59 us -> 6.03 us  [across(): return lax.ppermute(value, 'blk', [(i, i ^ mask) for i in range(owners)])]
    ppermute x7, starting transfers between devices: 11.3 us -> 12.3 us  [across(): return lax.ppermute(value, 'blk', [(i, i ^ mask) for i in range(owners)])]
  transfers between devices with their start and end apart: 15 -> 15, of which waited for: 10 -> 6; matrix products, arithmetic and copies ran while one was open for 0% -> 0% of each run, Pallas kernels for 0% -> 0%
where the time goes in v3:
time: 24.6 us; the launch traced here: 24.4 us
  starting transfers between devices  13.4 us (54%)
  waiting for transfers between devices  7.37 us (30%)
  Pallas kernels  3.57 us (15%)
    ppermute x7, starting transfers between devices, across(): return lax.ppermute(value, 'blk', [(i, i ^ mask) for i in range(owners)])  12.3 us
    ppermute x7, waiting for transfers between devices, across(): return lax.ppermute(value, 'blk', [(i, i ^ mask) for i in range(owners)])  6.03 us
    pallas_call x1, Pallas kernels, products(): pl.pallas_call(functools.partial(products_kernel, stored), out_shape=out,...  2.64 us
    ppermute x8, waiting for transfers between devices, gathered(): shards += [held[j], lax.ppermute(held[j], 'rhs', [(0, 1), (1, 0)])]  1.34 us
    ppermute x8, starting transfers between devices, gathered(): shards += [held[j], lax.ppermute(held[j], 'rhs', [(0, 1), (1, 0)])]  1.09 us
    pallas_call x1, Pallas kernels, load(): pl.pallas_call(load_kernel, out_shape=[pltpu.VMEM((2 * a.shape[0],) + a.s...  0.94 us
  transfers between devices with their start and end apart: 15, of which 6 were waited for; matrix products, arithmetic and copies ran while one was open for 0% of the time, Pallas kernels for 0%

profile of v3, /device:TPU:0, one launch (start us, length us, event | category | flops | bytes accessed | tf_op | source)
XLA Modules:
  0.0 24.4 jit_solution(12244318995318874173)
XLA Ops:
  0.0 0.9 %shard_map.55 = (bf16[16,16,256]{2,1,0:T(8,128)(2,1)S(1)}, s32[64]{0:T(128)S(4)}, s32[2,32]{1,0:T(2,128)S(4)}, s32[2,32]{1,0:T(2,128)S(4)}) custom-call(bf16[8,16,256]{2,1,0:T(8,128)(2,1)} %a.1, bf16[8,16,256]{2,1,0:T(8,128)(2,1)} %b.1, s32[64]{0:T(128)} %home.1, s32[2,32]{1,0:T(2,128)} %rows.1, s32[2,32]{1,0:T(2,128)} %cols.1), custom_call_target="tpu_custom_call" | custom-call | tf_op jit(solution)/shard_map/pallas_call | solution.py:96
  0.9 5.1 %collective-permute-start.7 = (bf16[16,16,256]{2,1,0:T(8,128)(2,1)S(1)}, bf16[16,16,256]{2,1,0:T(8,128)(2,1)S(1)}, u32[]{:S(2)}, u32[]{:S(2)}) collective-permute-start(bf16[16,16,256]{2,1,0:T(8,128)(2,1)S(1)} %get-tuple-element.9.refs_0_), channel_id=1, source_target_pairs={{0,12},{2,14},{4,8},{6,10},{8,4},{10,6},{12,0},{14,2},{1,13},{3,15... | collective-permute-start | bytes 393224 | tf_op jit(solution)/shard_map/ppermute | solution.py:179
  6.1 0.0 collective-permute-start.3
  6.1 1.5 %collective-permute-start.1 = (bf16[16,16,256]{2,1,0:T(8,128)(2,1)S(1)}, bf16[16,16,256]{2,1,0:T(8,128)(2,1)S(1)}, u32[]{:S(2)}, u32[]{:S(2)}) collective-permute-start(bf16[16,16,256]{2,1,0:T(8,128)(2,1)S(1)} %get-tuple-element.9.refs_0_), channel_id=1, source_target_pairs={{0,2},{2,0},{4,6},{6,4},{8,10},{10,8},{12,14},{14,12},{1,3},{3,1},... | collective-permute-start | bytes 393224 | tf_op jit(solution)/shard_map/ppermute | solution.py:179
  7.6 0.0 collective-permute-start
  7.6 2.9 %collective-permute-done.7.refs_12_ = bf16[16,16,256]{2,1,0:T(8,128)(2,1)S(1)} collective-permute-done((bf16[16,16,256]{2,1,0:T(8,128)(2,1)S(1)}, bf16[16,16,256]{2,1,0:T(8,128)(2,1)S(1)}, u32[]{:S(2)}, u32[]{:S(2)}) %collective-permute-start.7) | collective-permute-done | bytes 131104 | tf_op jit(solution)/shard_map/ppermute | solution.py:179
  10.4 1.6 %collective-permute-start.8 = (bf16[16,16,256]{2,1,0:T(8,128)(2,1)S(1)}, bf16[16,16,256]{2,1,0:T(8,128)(2,1)S(1)}, u32[]{:S(2)}, u32[]{:S(2)}) collective-permute-start(bf16[16,16,256]{2,1,0:T(8,128)(2,1)S(1)} %collective-permute-done.7.refs_12_), channel_id=1, source_target_pairs={{0,4},{2,6},{4,0},{6,2},{8,12},{10,14},{12,8},{14,10},{1,5},{3,7},... | collective-permute-start | bytes 393224 | tf_op jit(solution)/shard_map/ppermute | solution.py:179
  12.1 1.5 %collective-permute-start.13 = (bf16[16,16,256]{2,1,0:T(8,128)(2,1)S(1)}, bf16[16,16,256]{2,1,0:T(8,128)(2,1)S(1)}, u32[]{:S(2)}, u32[]{:S(2)}) collective-permute-start(bf16[16,16,256]{2,1,0:T(8,128)(2,1)S(1)} %collective-permute-done.7.refs_12_), channel_id=1, source_target_pairs={{0,2},{2,0},{4,6},{6,4},{8,10},{10,8},{12,14},{14,12},{1,3},{3,1},... | collective-permute-start | bytes 393224 | tf_op jit(solution)/shard_map/ppermute | solution.py:179
  13.6 0.0 collective-permute-done.3.refs_4_
  13.6 0.0 collective-permute-start.12
  13.6 0.0 collective-permute-done.1.refs_2_
  13.6 0.5 %collective-permute-start.4 = (bf16[16,16,256]{2,1,0:T(8,128)(2,1)S(1)}, bf16[16,16,256]{2,1,0:T(8,128)(2,1)S(1)}, u32[]{:S(2)}, u32[]{:S(2)}) collective-permute-start(bf16[16,16,256]{2,1,0:T(8,128)(2,1)S(1)} %collective-permute-done.3.refs_4_), channel_id=1, source_target_pairs={{0,1},{1,0},{2,3},{3,2},{4,5},{5,4},{6,7},{7,6},{8,9},{9,8},{10,11... | collective-permute-start | bytes 393224 | tf_op jit(solution)/shard_map/ppermute | solution.py:187
  14.1 0.0 collective-permute-done.refs_1_
  14.1 0.8 %collective-permute-start.5 = (bf16[16,16,256]{2,1,0:T(8,128)(2,1)S(1)}, bf16[16,16,256]{2,1,0:T(8,128)(2,1)S(1)}, u32[]{:S(2)}, u32[]{:S(2)}) collective-permute-start(bf16[16,16,256]{2,1,0:T(8,128)(2,1)S(1)} %collective-permute-done.1.refs_2_), channel_id=1, source_target_pairs={{0,4},{2,6},{4,0},{6,2},{8,12},{10,14},{12,8},{14,10},{1,5},{3,7},... | collective-permute-start | bytes 393224 | tf_op jit(solution)/shard_map/ppermute | solution.py:179
  14.9 0.5 %collective-permute-done.8.refs_8_ = bf16[16,16,256]{2,1,0:T(8,128)(2,1)S(1)} collective-permute-done((bf16[16,16,256]{2,1,0:T(8,128)(2,1)S(1)}, bf16[16,16,256]{2,1,0:T(8,128)(2,1)S(1)}, u32[]{:S(2)}, u32[]{:S(2)}) %collective-permute-start.8) | collective-permute-done | bytes 131104 | tf_op jit(solution)/shard_map/ppermute | solution.py:179
  15.4 1.7 %collective-permute-start.10 = (bf16[16,16,256]{2,1,0:T(8,128)(2,1)S(1)}, bf16[16,16,256]{2,1,0:T(8,128)(2,1)S(1)}, u32[]{:S(2)}, u32[]{:S(2)}) collective-permute-start(bf16[16,16,256]{2,1,0:T(8,128)(2,1)S(1)} %collective-permute-done.8.refs_8_), channel_id=1, source_target_pairs={{0,2},{2,0},{4,6},{6,4},{8,10},{10,8},{12,14},{14,12},{1,3},{3,1},... | collective-permute-start | bytes 393224 | tf_op jit(solution)/shard_map/ppermute | solution.py:179
  17.1 0.0 collective-permute-done.13.refs_14_
  17.1 0.0 collective-permute-start.2
  17.1 0.0 collective-permute-done.12.refs_13_
  17.1 0.5 %collective-permute-start.9 = (bf16[16,16,256]{2,1,0:T(8,128)(2,1)S(1)}, bf16[16,16,256]{2,1,0:T(8,128)(2,1)S(1)}, u32[]{:S(2)}, u32[]{:S(2)}) collective-permute-start(bf16[16,16,256]{2,1,0:T(8,128)(2,1)S(1)} %collective-permute-done.8.refs_8_), channel_id=1, source_target_pairs={{0,1},{1,0},{2,3},{3,2},{4,5},{5,4},{6,7},{7,6},{8,9},{9,8},{10,11... | collective-permute-start | bytes 393224 | tf_op jit(solution)/shard_map/ppermute | solution.py:187
  17.6 0.0 collective-permute-done.4.refs_5_
  17.6 0.1 collective-permute-start.14
  17.7 1.9 %collective-permute-done.5.refs_6_ = bf16[16,16,256]{2,1,0:T(8,128)(2,1)S(1)} collective-permute-done((bf16[16,16,256]{2,1,0:T(8,128)(2,1)S(1)}, bf16[16,16,256]{2,1,0:T(8,128)(2,1)S(1)}, u32[]{:S(2)}, u32[]{:S(2)}) %collective-permute-start.5) | collective-permute-done | bytes 131104 | tf_op jit(solution)/shard_map/ppermute | solution.py:179
  19.6 0.0 collective-permute-start.6
  19.6 0.8 %collective-permute-done.10.refs_10_ = bf16[16,16,256]{2,1,0:T(8,128)(2,1)S(1)} collective-permute-done((bf16[16,16,256]{2,1,0:T(8,128)(2,1)S(1)}, bf16[16,16,256]{2,1,0:T(8,128)(2,1)S(1)}, u32[]{:S(2)}, u32[]{:S(2)}) %collective-permute-start.10) | collective-permute-done | bytes 131104 | tf_op jit(solution)/shard_map/ppermute | solution.py:179
  20.4 0.0 collective-permute-start.11
  20.4 0.0 collective-permute-done.2.refs_3_
  20.4 0.0 collective-permute-done.14.refs_15_
  20.4 0.0 collective-permute-done.9.refs_9_
  20.4 0.5 %collective-permute-done.6.refs_7_ = bf16[16,16,256]{2,1,0:T(8,128)(2,1)S(1)} collective-permute-done((bf16[16,16,256]{2,1,0:T(8,128)(2,1)S(1)}, bf16[16,16,256]{2,1,0:T(8,128)(2,1)S(1)}, u32[]{:S(2)}, u32[]{:S(2)}) %collective-permute-start.6) | collective-permute-done | bytes 131104 | tf_op jit(solution)/shard_map/ppermute | solution.py:187
  20.9 0.8 %collective-permute-done.11.refs_11_ = bf16[16,16,256]{2,1,0:T(8,128)(2,1)S(1)} collective-permute-done((bf16[16,16,256]{2,1,0:T(8,128)(2,1)S(1)}, bf16[16,16,256]{2,1,0:T(8,128)(2,1)S(1)}, u32[]{:S(2)}, u32[]{:S(2)}) %collective-permute-start.11) | collective-permute-done | bytes 131104 | tf_op jit(solution)/shard_map/ppermute | solution.py:187
  21.7 2.6 %shard_map.56 = bf16[64,128,256]{2,1,0:T(8,128)(2,1)} custom-call(bf16[16,16,256]{2,1,0:T(8,128)(2,1)S(1)} %get-tuple-element.9.refs_0_, bf16[16,16,256]{2,1,0:T(8,128)(2,1)S(1)} %collective-permute-done.refs_1_, bf16[16,16,256]{2,1,0:T(8,128)(2,1)S(1)} %collective-permute-done.1.refs_2_, bf16[16,16,256]{2,1,0:T(8,128)(2,1)S(1)} %collective-permute-done.2.refs_3_, ...), custom_call_target="tpu_custom_call" | custom-call | tf_op jit(solution)/shard_map/pallas_call | solution.py:157
Async XLA Ops:
  0.9 9.5 %collective-permute-start.7 = (bf16[16,16,256]{2,1,0:T(8,128)(2,1)S(1)}, bf16[16,16,256]{2,1,0:T(8,128)(2,1)S(1)}, u32[]{:S(2)}, u32[]{:S(2)}) collective-permute-start(bf16[16,16,256]{2,1,0:T(8,128)(2,1)S(1)} %get-tuple-element.9.refs_0_), channel_id=1, source_target_pairs={{0,12},{2,14},{4,8},{6,10},{8,4},{10,6},{12,0},{14,2},{1,13},{3,15... | collective-permute-start | bytes 393224 | tf_op jit(solution)/shard_map/ppermute | solution.py:179
  6.1 7.5 %collective-permute-start.3 = (bf16[16,16,256]{2,1,0:T(8,128)(2,1)S(1)}, bf16[16,16,256]{2,1,0:T(8,128)(2,1)S(1)}, u32[]{:S(2)}, u32[]{:S(2)}) collective-permute-start(bf16[16,16,256]{2,1,0:T(8,128)(2,1)S(1)} %get-tuple-element.9.refs_0_), channel_id=1, source_target_pairs={{0,4},{2,6},{4,0},{6,2},{8,12},{10,14},{12,8},{14,10},{1,5},{3,7},... | collective-permute-start | bytes 393224 | tf_op jit(solution)/shard_map/ppermute | solution.py:179
  6.1 7.5 %collective-permute-start.1 = (bf16[16,16,256]{2,1,0:T(8,128)(2,1)S(1)}, bf16[16,16,256]{2,1,0:T(8,128)(2,1)S(1)}, u32[]{:S(2)}, u32[]{:S(2)}) collective-permute-start(bf16[16,16,256]{2,1,0:T(8,128)(2,1)S(1)} %get-tuple-element.9.refs_0_), channel_id=1, source_target_pairs={{0,2},{2,0},{4,6},{6,4},{8,10},{10,8},{12,14},{14,12},{1,3},{3,1},... | collective-permute-start | bytes 393224 | tf_op jit(solution)/shard_map/ppermute | solution.py:179
  7.6 6.5 %collective-permute-start = (bf16[16,16,256]{2,1,0:T(8,128)(2,1)S(1)}, bf16[16,16,256]{2,1,0:T(8,128)(2,1)S(1)}, u32[]{:S(2)}, u32[]{:S(2)}) collective-permute-start(bf16[16,16,256]{2,1,0:T(8,128)(2,1)S(1)} %get-tuple-element.9.refs_0_), channel_id=1, source_target_pairs={{0,1},{1,0},{2,3},{3,2},{4,5},{5,4},{6,7},{7,6},{8,9},{9,8},{10,11... | collective-permute-start | bytes 393224 | tf_op jit(solution)/shard_map/ppermute | solution.py:187
  10.4 5.0 %collective-permute-start.8 = (bf16[16,16,256]{2,1,0:T(8,128)(2,1)S(1)}, bf16[16,16,256]{2,1,0:T(8,128)(2,1)S(1)}, u32[]{:S(2)}, u32[]{:S(2)}) collective-permute-start(bf16[16,16,256]{2,1,0:T(8,128)(2,1)S(1)} %collective-permute-done.7.refs_12_), channel_id=1, source_target_pairs={{0,4},{2,6},{4,0},{6,2},{8,12},{10,14},{12,8},{14,10},{1,5},{3,7},... | collective-permute-start | bytes 393224 | tf_op jit(solution)/shard_map/ppermute | solution.py:179
  12.1 5.0 %collective-permute-start.13 = (bf16[16,16,256]{2,1,0:T(8,128)(2,1)S(1)}, bf16[16,16,256]{2,1,0:T(8,128)(2,1)S(1)}, u32[]{:S(2)}, u32[]{:S(2)}) collective-permute-start(bf16[16,16,256]{2,1,0:T(8,128)(2,1)S(1)} %collective-permute-done.7.refs_12_), channel_id=1, source_target_pairs={{0,2},{2,0},{4,6},{6,4},{8,10},{10,8},{12,14},{14,12},{1,3},{3,1},... | collective-permute-start | bytes 393224 | tf_op jit(solution)/shard_map/ppermute | solution.py:179
  13.6 3.5 %collective-permute-start.12 = (bf16[16,16,256]{2,1,0:T(8,128)(2,1)S(1)}, bf16[16,16,256]{2,1,0:T(8,128)(2,1)S(1)}, u32[]{:S(2)}, u32[]{:S(2)}) collective-permute-start(bf16[16,16,256]{2,1,0:T(8,128)(2,1)S(1)} %collective-permute-done.7.refs_12_), channel_id=1, source_target_pairs={{0,1},{1,0},{2,3},{3,2},{4,5},{5,4},{6,7},{7,6},{8,9},{9,8},{10,11... | collective-permute-start | bytes 393224 | tf_op jit(solution)/shard_map/ppermute | solution.py:187
  13.6 4.0 %collective-permute-start.4 = (bf16[16,16,256]{2,1,0:T(8,128)(2,1)S(1)}, bf16[16,16,256]{2,1,0:T(8,128)(2,1)S(1)}, u32[]{:S(2)}, u32[]{:S(2)}) collective-permute-start(bf16[16,16,256]{2,1,0:T(8,128)(2,1)S(1)} %collective-permute-done.3.refs_4_), channel_id=1, source_target_pairs={{0,1},{1,0},{2,3},{3,2},{4,5},{5,4},{6,7},{7,6},{8,9},{9,8},{10,11... | collective-permute-start | bytes 393224 | tf_op jit(solution)/shard_map/ppermute | solution.py:187
  14.1 5.5 %collective-permute-start.5 = (bf16[16,16,256]{2,1,0:T(8,128)(2,1)S(1)}, bf16[16,16,256]{2,1,0:T(8,128)(2,1)S(1)}, u32[]{:S(2)}, u32[]{:S(2)}) collective-permute-start(bf16[16,16,256]{2,1,0:T(8,128)(2,1)S(1)} %collective-permute-done.1.refs_2_), channel_id=1, source_target_pairs={{0,4},{2,6},{4,0},{6,2},{8,12},{10,14},{12,8},{14,10},{1,5},{3,7},... | collective-permute-start | bytes 393224 | tf_op jit(solution)/shard_map/ppermute | solution.py:179
  15.4 5.0 %collective-permute-start.10 = (bf16[16,16,256]{2,1,0:T(8,128)(2,1)S(1)}, bf16[16,16,256]{2,1,0:T(8,128)(2,1)S(1)}, u32[]{:S(2)}, u32[]{:S(2)}) collective-permute-start(bf16[16,16,256]{2,1,0:T(8,128)(2,1)S(1)} %collective-permute-done.8.refs_8_), channel_id=1, source_target_pairs={{0,2},{2,0},{4,6},{6,4},{8,10},{10,8},{12,14},{14,12},{1,3},{3,1},... | collective-permute-start | bytes 393224 | tf_op jit(solution)/shard_map/ppermute | solution.py:179
  17.1 3.3 %collective-permute-start.2 = (bf16[16,16,256]{2,1,0:T(8,128)(2,1)S(1)}, bf16[16,16,256]{2,1,0:T(8,128)(2,1)S(1)}, u32[]{:S(2)}, u32[]{:S(2)}) collective-permute-start(bf16[16,16,256]{2,1,0:T(8,128)(2,1)S(1)} %collective-permute-done.1.refs_2_), channel_id=1, source_target_pairs={{0,1},{1,0},{2,3},{3,2},{4,5},{5,4},{6,7},{7,6},{8,9},{9,8},{10,11... | collective-permute-start | bytes 393224 | tf_op jit(solution)/shard_map/ppermute | solution.py:187
  17.1 3.3 %collective-permute-start.9 = (bf16[16,16,256]{2,1,0:T(8,128)(2,1)S(1)}, bf16[16,16,256]{2,1,0:T(8,128)(2,1)S(1)}, u32[]{:S(2)}, u32[]{:S(2)}) collective-permute-start(bf16[16,16,256]{2,1,0:T(8,128)(2,1)S(1)} %collective-permute-done.8.refs_8_), channel_id=1, source_target_pairs={{0,1},{1,0},{2,3},{3,2},{4,5},{5,4},{6,7},{7,6},{8,9},{9,8},{10,11... | collective-permute-start | bytes 393224 | tf_op jit(solution)/shard_map/ppermute | solution.py:187
  17.6 2.8 %collective-permute-start.14 = (bf16[16,16,256]{2,1,0:T(8,128)(2,1)S(1)}, bf16[16,16,256]{2,1,0:T(8,128)(2,1)S(1)}, u32[]{:S(2)}, u32[]{:S(2)}) collective-permute-start(bf16[16,16,256]{2,1,0:T(8,128)(2,1)S(1)} %collective-permute-done.13.refs_14_), channel_id=1, source_target_pairs={{0,1},{1,0},{2,3},{3,2},{4,5},{5,4},{6,7},{7,6},{8,9},{9,8},{10,11... | collective-permute-start | bytes 393224 | tf_op jit(solution)/shard_map/ppermute | solution.py:187
  19.6 1.3 %collective-permute-start.6 = (bf16[16,16,256]{2,1,0:T(8,128)(2,1)S(1)}, bf16[16,16,256]{2,1,0:T(8,128)(2,1)S(1)}, u32[]{:S(2)}, u32[]{:S(2)}) collective-permute-start(bf16[16,16,256]{2,1,0:T(8,128)(2,1)S(1)} %collective-permute-done.5.refs_6_), channel_id=1, source_target_pairs={{0,1},{1,0},{2,3},{3,2},{4,5},{5,4},{6,7},{7,6},{8,9},{9,8},{10,11... | collective-permute-start | bytes 393224 | tf_op jit(solution)/shard_map/ppermute | solution.py:187
  20.4 1.3 %collective-permute-start.11 = (bf16[16,16,256]{2,1,0:T(8,128)(2,1)S(1)}, bf16[16,16,256]{2,1,0:T(8,128)(2,1)S(1)}, u32[]{:S(2)}, u32[]{:S(2)}) collective-permute-start(bf16[16,16,256]{2,1,0:T(8,128)(2,1)S(1)} %collective-permute-done.10.refs_10_), channel_id=1, source_target_pairs={{0,1},{1,0},{2,3},{3,2},{4,5},{5,4},{6,7},{7,6},{8,9},{9,8},{10,11... | collective-permute-start | bytes 393224 | tf_op jit(solution)/shard_map/ppermute | solution.py:187

commit v4 on v3

--- a/solution.py
+++ b/solution.py
@@ -139,7 +139,8 @@
                 out_copy(strip * (per_strip // CHUNK) + k // CHUNK).start()
         return carry
 
-    lax.fori_loop(0, strips, one_strip, 0)
+    for strip in range(strips):
+        one_strip(strip, 0)
 
     def drain(n, carry):
         out_copy(n).wait()

time: 24.6 us -> 24.5 us (level)
  no operation moved by 1% of the time
where the time goes in v4:
time: 24.5 us; the launch traced here: 24.2 us
  starting transfers between devices  13.4 us (55%)
  waiting for transfers between devices  7.37 us (30%)
  Pallas kernels  3.43 us (14%)
    ppermute x7, starting transfers between devices, across(): return lax.ppermute(value, 'blk', [(i, i ^ mask) for i in range(owners)])  12.3 us
    ppermute x7, waiting for transfers between devices, across(): return lax.ppermute(value, 'blk', [(i, i ^ mask) for i in range(owners)])  6.03 us
    pallas_call x1, Pallas kernels, products(): pl.pallas_call(functools.partial(products_kernel, stored), out_shape=out,...  2.49 us
    ppermute x8, waiting for transfers between devices, gathered(): shards += [held[j], lax.ppermute(held[j], 'rhs', [(0, 1), (1, 0)])]  1.34 us
    ppermute x8, starting transfers between devices, gathered(): shards += [held[j], lax.ppermute(held[j], 'rhs', [(0, 1), (1, 0)])]  1.09 us
    pallas_call x1, Pallas kernels, load(): pl.pallas_call(load_kernel, out_shape=[pltpu.VMEM((2 * a.shape[0],) + a.s...  0.94 us
  transfers between devices with their start and end apart: 15, of which 6 were waited for; matrix products, arithmetic and copies ran while one was open for 0% of the time, Pallas kernels for 0%

profile of v4, /device:TPU:0, one launch (start us, length us, event | category | flops | bytes accessed | tf_op | source)
XLA Modules:
  0.0 24.2 jit_solution(10030479965107161272)
XLA Ops:
  0.0 0.9 %shard_map.55 = (bf16[16,16,256]{2,1,0:T(8,128)(2,1)S(1)}, s32[64]{0:T(128)S(4)}, s32[2,32]{1,0:T(2,128)S(4)}, s32[2,32]{1,0:T(2,128)S(4)}) custom-call(bf16[8,16,256]{2,1,0:T(8,128)(2,1)} %a.1, bf16[8,16,256]{2,1,0:T(8,128)(2,1)} %b.1, s32[64]{0:T(128)} %home.1, s32[2,32]{1,0:T(2,128)} %rows.1, s32[2,32]{1,0:T(2,128)} %cols.1), custom_call_target="tpu_custom_call" | custom-call | tf_op jit(solution)/shard_map/pallas_call | solution.py:96
  0.9 5.1 %collective-permute-start.7 = (bf16[16,16,256]{2,1,0:T(8,128)(2,1)S(1)}, bf16[16,16,256]{2,1,0:T(8,128)(2,1)S(1)}, u32[]{:S(2)}, u32[]{:S(2)}) collective-permute-start(bf16[16,16,256]{2,1,0:T(8,128)(2,1)S(1)} %get-tuple-element.9.refs_0_), channel_id=1, source_target_pairs={{0,12},{2,14},{4,8},{6,10},{8,4},{10,6},{12,0},{14,2},{1,13},{3,15... | collective-permute-start | bytes 393224 | tf_op jit(solution)/shard_map/ppermute | solution.py:180
  6.1 0.0 collective-permute-start.3
  6.1 1.5 %collective-permute-start.1 = (bf16[16,16,256]{2,1,0:T(8,128)(2,1)S(1)}, bf16[16,16,256]{2,1,0:T(8,128)(2,1)S(1)}, u32[]{:S(2)}, u32[]{:S(2)}) collective-permute-start(bf16[16,16,256]{2,1,0:T(8,128)(2,1)S(1)} %get-tuple-element.9.refs_0_), channel_id=1, source_target_pairs={{0,2},{2,0},{4,6},{6,4},{8,10},{10,8},{12,14},{14,12},{1,3},{3,1},... | collective-permute-start | bytes 393224 | tf_op jit(solution)/shard_map/ppermute | solution.py:180
  7.6 0.0 collective-permute-start
  7.6 2.9 %collective-permute-done.7.refs_12_ = bf16[16,16,256]{2,1,0:T(8,128)(2,1)S(1)} collective-permute-done((bf16[16,16,256]{2,1,0:T(8,128)(2,1)S(1)}, bf16[16,16,256]{2,1,0:T(8,128)(2,1)S(1)}, u32[]{:S(2)}, u32[]{:S(2)}) %collective-permute-start.7) | collective-permute-done | bytes 131104 | tf_op jit(solution)/shard_map/ppermute | solution.py:180
  10.4 1.6 %collective-permute-start.8 = (bf16[16,16,256]{2,1,0:T(8,128)(2,1)S(1)}, bf16[16,16,256]{2,1,0:T(8,128)(2,1)S(1)}, u32[]{:S(2)}, u32[]{:S(2)}) collective-permute-start(bf16[16,16,256]{2,1,0:T(8,128)(2,1)S(1)} %collective-permute-done.7.refs_12_), channel_id=1, source_target_pairs={{0,4},{2,6},{4,0},{6,2},{8,12},{10,14},{12,8},{14,10},{1,5},{3,7},... | collective-permute-start | bytes 393224 | tf_op jit(solution)/shard_map/ppermute | solution.py:180
  12.1 1.5 %collective-permute-start.13 = (bf16[16,16,256]{2,1,0:T(8,128)(2,1)S(1)}, bf16[16,16,256]{2,1,0:T(8,128)(2,1)S(1)}, u32[]{:S(2)}, u32[]{:S(2)}) collective-permute-start(bf16[16,16,256]{2,1,0:T(8,128)(2,1)S(1)} %collective-permute-done.7.refs_12_), channel_id=1, source_target_pairs={{0,2},{2,0},{4,6},{6,4},{8,10},{10,8},{12,14},{14,12},{1,3},{3,1},... | collective-permute-start | bytes 393224 | tf_op jit(solution)/shard_map/ppermute | solution.py:180
  13.6 0.0 collective-permute-done.3.refs_4_
  13.6 0.0 collective-permute-start.12
  13.6 0.0 collective-permute-done.1.refs_2_
  13.6 0.5 %collective-permute-start.4 = (bf16[16,16,256]{2,1,0:T(8,128)(2,1)S(1)}, bf16[16,16,256]{2,1,0:T(8,128)(2,1)S(1)}, u32[]{:S(2)}, u32[]{:S(2)}) collective-permute-start(bf16[16,16,256]{2,1,0:T(8,128)(2,1)S(1)} %collective-permute-done.3.refs_4_), channel_id=1, source_target_pairs={{0,1},{1,0},{2,3},{3,2},{4,5},{5,4},{6,7},{7,6},{8,9},{9,8},{10,11... | collective-permute-start | bytes 393224 | tf_op jit(solution)/shard_map/ppermute | solution.py:188
  14.1 0.0 collective-permute-done.refs_1_
  14.1 0.8 %collective-permute-start.5 = (bf16[16,16,256]{2,1,0:T(8,128)(2,1)S(1)}, bf16[16,16,256]{2,1,0:T(8,128)(2,1)S(1)}, u32[]{:S(2)}, u32[]{:S(2)}) collective-permute-start(bf16[16,16,256]{2,1,0:T(8,128)(2,1)S(1)} %collective-permute-done.1.refs_2_), channel_id=1, source_target_pairs={{0,4},{2,6},{4,0},{6,2},{8,12},{10,14},{12,8},{14,10},{1,5},{3,7},... | collective-permute-start | bytes 393224 | tf_op jit(solution)/shard_map/ppermute | solution.py:180
  14.9 0.5 %collective-permute-done.8.refs_8_ = bf16[16,16,256]{2,1,0:T(8,128)(2,1)S(1)} collective-permute-done((bf16[16,16,256]{2,1,0:T(8,128)(2,1)S(1)}, bf16[16,16,256]{2,1,0:T(8,128)(2,1)S(1)}, u32[]{:S(2)}, u32[]{:S(2)}) %collective-permute-start.8) | collective-permute-done | bytes 131104 | tf_op jit(solution)/shard_map/ppermute | solution.py:180
  15.4 1.7 %collective-permute-start.10 = (bf16[16,16,256]{2,1,0:T(8,128)(2,1)S(1)}, bf16[16,16,256]{2,1,0:T(8,128)(2,1)S(1)}, u32[]{:S(2)}, u32[]{:S(2)}) collective-permute-start(bf16[16,16,256]{2,1,0:T(8,128)(2,1)S(1)} %collective-permute-done.8.refs_8_), channel_id=1, source_target_pairs={{0,2},{2,0},{4,6},{6,4},{8,10},{10,8},{12,14},{14,12},{1,3},{3,1},... | collective-permute-start | bytes 393224 | tf_op jit(solution)/shard_map/ppermute | solution.py:180
  17.1 0.0 collective-permute-done.13.refs_14_
  17.1 0.0 collective-permute-start.2
  17.1 0.0 collective-permute-done.12.refs_13_
  17.1 0.5 %collective-permute-start.9 = (bf16[16,16,256]{2,1,0:T(8,128)(2,1)S(1)}, bf16[16,16,256]{2,1,0:T(8,128)(2,1)S(1)}, u32[]{:S(2)}, u32[]{:S(2)}) collective-permute-start(bf16[16,16,256]{2,1,0:T(8,128)(2,1)S(1)} %collective-permute-done.8.refs_8_), channel_id=1, source_target_pairs={{0,1},{1,0},{2,3},{3,2},{4,5},{5,4},{6,7},{7,6},{8,9},{9,8},{10,11... | collective-permute-start | bytes 393224 | tf_op jit(solution)/shard_map/ppermute | solution.py:188
  17.6 0.0 collective-permute-done.4.refs_5_
  17.6 0.1 collective-permute-start.14
  17.7 1.9 %collective-permute-done.5.refs_6_ = bf16[16,16,256]{2,1,0:T(8,128)(2,1)S(1)} collective-permute-done((bf16[16,16,256]{2,1,0:T(8,128)(2,1)S(1)}, bf16[16,16,256]{2,1,0:T(8,128)(2,1)S(1)}, u32[]{:S(2)}, u32[]{:S(2)}) %collective-permute-start.5) | collective-permute-done | bytes 131104 | tf_op jit(solution)/shard_map/ppermute | solution.py:180
  19.6 0.0 collective-permute-start.6
  19.6 0.8 %collective-permute-done.10.refs_10_ = bf16[16,16,256]{2,1,0:T(8,128)(2,1)S(1)} collective-permute-done((bf16[16,16,256]{2,1,0:T(8,128)(2,1)S(1)}, bf16[16,16,256]{2,1,0:T(8,128)(2,1)S(1)}, u32[]{:S(2)}, u32[]{:S(2)}) %collective-permute-start.10) | collective-permute-done | bytes 131104 | tf_op jit(solution)/shard_map/ppermute | solution.py:180
  20.4 0.0 collective-permute-start.11
  20.4 0.0 collective-permute-done.2.refs_3_
  20.4 0.0 collective-permute-done.14.refs_15_
  20.4 0.0 collective-permute-done.9.refs_9_
  20.4 0.5 %collective-permute-done.6.refs_7_ = bf16[16,16,256]{2,1,0:T(8,128)(2,1)S(1)} collective-permute-done((bf16[16,16,256]{2,1,0:T(8,128)(2,1)S(1)}, bf16[16,16,256]{2,1,0:T(8,128)(2,1)S(1)}, u32[]{:S(2)}, u32[]{:S(2)}) %collective-permute-start.6) | collective-permute-done | bytes 131104 | tf_op jit(solution)/shard_map/ppermute | solution.py:188
  20.9 0.8 %collective-permute-done.11.refs_11_ = bf16[16,16,256]{2,1,0:T(8,128)(2,1)S(1)} collective-permute-done((bf16[16,16,256]{2,1,0:T(8,128)(2,1)S(1)}, bf16[16,16,256]{2,1,0:T(8,128)(2,1)S(1)}, u32[]{:S(2)}, u32[]{:S(2)}) %collective-permute-start.11) | collective-permute-done | bytes 131104 | tf_op jit(solution)/shard_map/ppermute | solution.py:188
  21.7 2.5 %shard_map.56 = bf16[64,128,256]{2,1,0:T(8,128)(2,1)} custom-call(bf16[16,16,256]{2,1,0:T(8,128)(2,1)S(1)} %get-tuple-element.9.refs_0_, bf16[16,16,256]{2,1,0:T(8,128)(2,1)S(1)} %collective-permute-done.refs_1_, bf16[16,16,256]{2,1,0:T(8,128)(2,1)S(1)} %collective-permute-done.1.refs_2_, bf16[16,16,256]{2,1,0:T(8,128)(2,1)S(1)} %collective-permute-done.2.refs_3_, ...), custom_call_target="tpu_custom_call" | custom-call | tf_op jit(solution)/shard_map/pallas_call | solution.py:158
Async XLA Ops:
  0.9 9.5 %collective-permute-start.7 = (bf16[16,16,256]{2,1,0:T(8,128)(2,1)S(1)}, bf16[16,16,256]{2,1,0:T(8,128)(2,1)S(1)}, u32[]{:S(2)}, u32[]{:S(2)}) collective-permute-start(bf16[16,16,256]{2,1,0:T(8,128)(2,1)S(1)} %get-tuple-element.9.refs_0_), channel_id=1, source_target_pairs={{0,12},{2,14},{4,8},{6,10},{8,4},{10,6},{12,0},{14,2},{1,13},{3,15... | collective-permute-start | bytes 393224 | tf_op jit(solution)/shard_map/ppermute | solution.py:180
  6.1 7.5 %collective-permute-start.3 = (bf16[16,16,256]{2,1,0:T(8,128)(2,1)S(1)}, bf16[16,16,256]{2,1,0:T(8,128)(2,1)S(1)}, u32[]{:S(2)}, u32[]{:S(2)}) collective-permute-start(bf16[16,16,256]{2,1,0:T(8,128)(2,1)S(1)} %get-tuple-element.9.refs_0_), channel_id=1, source_target_pairs={{0,4},{2,6},{4,0},{6,2},{8,12},{10,14},{12,8},{14,10},{1,5},{3,7},... | collective-permute-start | bytes 393224 | tf_op jit(solution)/shard_map/ppermute | solution.py:180
  6.1 7.5 %collective-permute-start.1 = (bf16[16,16,256]{2,1,0:T(8,128)(2,1)S(1)}, bf16[16,16,256]{2,1,0:T(8,128)(2,1)S(1)}, u32[]{:S(2)}, u32[]{:S(2)}) collective-permute-start(bf16[16,16,256]{2,1,0:T(8,128)(2,1)S(1)} %get-tuple-element.9.refs_0_), channel_id=1, source_target_pairs={{0,2},{2,0},{4,6},{6,4},{8,10},{10,8},{12,14},{14,12},{1,3},{3,1},... | collective-permute-start | bytes 393224 | tf_op jit(solution)/shard_map/ppermute | solution.py:180
  7.6 6.5 %collective-permute-start = (bf16[16,16,256]{2,1,0:T(8,128)(2,1)S(1)}, bf16[16,16,256]{2,1,0:T(8,128)(2,1)S(1)}, u32[]{:S(2)}, u32[]{:S(2)}) collective-permute-start(bf16[16,16,256]{2,1,0:T(8,128)(2,1)S(1)} %get-tuple-element.9.refs_0_), channel_id=1, source_target_pairs={{0,1},{1,0},{2,3},{3,2},{4,5},{5,4},{6,7},{7,6},{8,9},{9,8},{10,11... | collective-permute-start | bytes 393224 | tf_op jit(solution)/shard_map/ppermute | solution.py:188
  10.4 5.0 %collective-permute-start.8 = (bf16[16,16,256]{2,1,0:T(8,128)(2,1)S(1)}, bf16[16,16,256]{2,1,0:T(8,128)(2,1)S(1)}, u32[]{:S(2)}, u32[]{:S(2)}) collective-permute-start(bf16[16,16,256]{2,1,0:T(8,128)(2,1)S(1)} %collective-permute-done.7.refs_12_), channel_id=1, source_target_pairs={{0,4},{2,6},{4,0},{6,2},{8,12},{10,14},{12,8},{14,10},{1,5},{3,7},... | collective-permute-start | bytes 393224 | tf_op jit(solution)/shard_map/ppermute | solution.py:180
  12.1 5.0 %collective-permute-start.13 = (bf16[16,16,256]{2,1,0:T(8,128)(2,1)S(1)}, bf16[16,16,256]{2,1,0:T(8,128)(2,1)S(1)}, u32[]{:S(2)}, u32[]{:S(2)}) collective-permute-start(bf16[16,16,256]{2,1,0:T(8,128)(2,1)S(1)} %collective-permute-done.7.refs_12_), channel_id=1, source_target_pairs={{0,2},{2,0},{4,6},{6,4},{8,10},{10,8},{12,14},{14,12},{1,3},{3,1},... | collective-permute-start | bytes 393224 | tf_op jit(solution)/shard_map/ppermute | solution.py:180
  13.6 3.5 %collective-permute-start.12 = (bf16[16,16,256]{2,1,0:T(8,128)(2,1)S(1)}, bf16[16,16,256]{2,1,0:T(8,128)(2,1)S(1)}, u32[]{:S(2)}, u32[]{:S(2)}) collective-permute-start(bf16[16,16,256]{2,1,0:T(8,128)(2,1)S(1)} %collective-permute-done.7.refs_12_), channel_id=1, source_target_pairs={{0,1},{1,0},{2,3},{3,2},{4,5},{5,4},{6,7},{7,6},{8,9},{9,8},{10,11... | collective-permute-start | bytes 393224 | tf_op jit(solution)/shard_map/ppermute | solution.py:188
  13.6 4.0 %collective-permute-start.4 = (bf16[16,16,256]{2,1,0:T(8,128)(2,1)S(1)}, bf16[16,16,256]{2,1,0:T(8,128)(2,1)S(1)}, u32[]{:S(2)}, u32[]{:S(2)}) collective-permute-start(bf16[16,16,256]{2,1,0:T(8,128)(2,1)S(1)} %collective-permute-done.3.refs_4_), channel_id=1, source_target_pairs={{0,1},{1,0},{2,3},{3,2},{4,5},{5,4},{6,7},{7,6},{8,9},{9,8},{10,11... | collective-permute-start | bytes 393224 | tf_op jit(solution)/shard_map/ppermute | solution.py:188
  14.1 5.5 %collective-permute-start.5 = (bf16[16,16,256]{2,1,0:T(8,128)(2,1)S(1)}, bf16[16,16,256]{2,1,0:T(8,128)(2,1)S(1)}, u32[]{:S(2)}, u32[]{:S(2)}) collective-permute-start(bf16[16,16,256]{2,1,0:T(8,128)(2,1)S(1)} %collective-permute-done.1.refs_2_), channel_id=1, source_target_pairs={{0,4},{2,6},{4,0},{6,2},{8,12},{10,14},{12,8},{14,10},{1,5},{3,7},... | collective-permute-start | bytes 393224 | tf_op jit(solution)/shard_map/ppermute | solution.py:180
  15.4 5.0 %collective-permute-start.10 = (bf16[16,16,256]{2,1,0:T(8,128)(2,1)S(1)}, bf16[16,16,256]{2,1,0:T(8,128)(2,1)S(1)}, u32[]{:S(2)}, u32[]{:S(2)}) collective-permute-start(bf16[16,16,256]{2,1,0:T(8,128)(2,1)S(1)} %collective-permute-done.8.refs_8_), channel_id=1, source_target_pairs={{0,2},{2,0},{4,6},{6,4},{8,10},{10,8},{12,14},{14,12},{1,3},{3,1},... | collective-permute-start | bytes 393224 | tf_op jit(solution)/shard_map/ppermute | solution.py:180
  17.1 3.3 %collective-permute-start.2 = (bf16[16,16,256]{2,1,0:T(8,128)(2,1)S(1)}, bf16[16,16,256]{2,1,0:T(8,128)(2,1)S(1)}, u32[]{:S(2)}, u32[]{:S(2)}) collective-permute-start(bf16[16,16,256]{2,1,0:T(8,128)(2,1)S(1)} %collective-permute-done.1.refs_2_), channel_id=1, source_target_pairs={{0,1},{1,0},{2,3},{3,2},{4,5},{5,4},{6,7},{7,6},{8,9},{9,8},{10,11... | collective-permute-start | bytes 393224 | tf_op jit(solution)/shard_map/ppermute | solution.py:188
  17.1 3.3 %collective-permute-start.9 = (bf16[16,16,256]{2,1,0:T(8,128)(2,1)S(1)}, bf16[16,16,256]{2,1,0:T(8,128)(2,1)S(1)}, u32[]{:S(2)}, u32[]{:S(2)}) collective-permute-start(bf16[16,16,256]{2,1,0:T(8,128)(2,1)S(1)} %collective-permute-done.8.refs_8_), channel_id=1, source_target_pairs={{0,1},{1,0},{2,3},{3,2},{4,5},{5,4},{6,7},{7,6},{8,9},{9,8},{10,11... | collective-permute-start | bytes 393224 | tf_op jit(solution)/shard_map/ppermute | solution.py:188
  17.6 2.8 %collective-permute-start.14 = (bf16[16,16,256]{2,1,0:T(8,128)(2,1)S(1)}, bf16[16,16,256]{2,1,0:T(8,128)(2,1)S(1)}, u32[]{:S(2)}, u32[]{:S(2)}) collective-permute-start(bf16[16,16,256]{2,1,0:T(8,128)(2,1)S(1)} %collective-permute-done.13.refs_14_), channel_id=1, source_target_pairs={{0,1},{1,0},{2,3},{3,2},{4,5},{5,4},{6,7},{7,6},{8,9},{9,8},{10,11... | collective-permute-start | bytes 393224 | tf_op jit(solution)/shard_map/ppermute | solution.py:188
  19.6 1.3 %collective-permute-start.6 = (bf16[16,16,256]{2,1,0:T(8,128)(2,1)S(1)}, bf16[16,16,256]{2,1,0:T(8,128)(2,1)S(1)}, u32[]{:S(2)}, u32[]{:S(2)}) collective-permute-start(bf16[16,16,256]{2,1,0:T(8,128)(2,1)S(1)} %collective-permute-done.5.refs_6_), channel_id=1, source_target_pairs={{0,1},{1,0},{2,3},{3,2},{4,5},{5,4},{6,7},{7,6},{8,9},{9,8},{10,11... | collective-permute-start | bytes 393224 | tf_op jit(solution)/shard_map/ppermute | solution.py:188
  20.4 1.3 %collective-permute-start.11 = (bf16[16,16,256]{2,1,0:T(8,128)(2,1)S(1)}, bf16[16,16,256]{2,1,0:T(8,128)(2,1)S(1)}, u32[]{:S(2)}, u32[]{:S(2)}) collective-permute-start(bf16[16,16,256]{2,1,0:T(8,128)(2,1)S(1)} %collective-permute-done.10.refs_10_), channel_id=1, source_target_pairs={{0,1},{1,0},{2,3},{3,2},{4,5},{5,4},{6,7},{7,6},{8,9},{9,8},{10,11... | collective-permute-start | bytes 393224 | tf_op jit(solution)/shard_map/ppermute | solution.py:188

commit v5 on v4

--- a/solution.py
+++ b/solution.py
@@ -78,13 +78,11 @@
 
 def load_kernel(a, b, home, rows, cols, out, home_s, rows_s, cols_s, sem):
     n = a.shape[0]
-    pairs = (
-        (a, out.at[pl.ds(0, n)]),
-        (b, out.at[pl.ds(n, n)]),
-        (home, home_s),
-        (rows, rows_s),
-        (cols, cols_s),
-    )
+    size = n // 2
+    pairs = [(home, home_s), (rows, rows_s), (cols, cols_s)]
+    for k in range(2):
+        pairs.append((a.at[pl.ds(k * size, size)], out.at[pl.ds(k * size, size)]))
+        pairs.append((b.at[pl.ds(k * size, size)], out.at[pl.ds(n + k * size, size)]))
     copies = [pltpu.make_async_copy(*pair, sem.at[k]) for k, pair in enumerate(pairs)]
     for copy in copies:
         copy.start()
@@ -99,26 +97,28 @@
         + [pltpu.SMEM(v.shape, v.dtype) for v in index],
         in_specs=[ANY] * 5,
         out_specs=[VMEM] + [SMEM] * 3,
-        scratch_shapes=[pltpu.SemaphoreType.DMA((5,))],
+        scratch_shapes=[pltpu.SemaphoreType.DMA((7,))],
         compiler_params=pltpu.CompilerParams(vmem_limit_bytes=1 << 20),
     )(*(pltpu.with_memory_space_constraint(v, pltpu.HBM) for v in (a, b) + index))
 
 
-def stage(shards, left, right):
+def stage(masks, shards, left, right):
     joined, rhs, _ = shards[0].shape
     stored, half = joined // 2, left.shape[2]
-    start = pl.multiple_of(lax.axis_index("rhs") * half, half)
+    core = lax.axis_index("rhs")
+    start = pl.multiple_of(core * half, half)
     for n, shard in enumerate(shards):
-        slots = slice(n // 2 * stored, (n // 2 + 1) * stored)
+        mine, other = masks[n // 2] if n % 2 == 0 else masks[n // 2][::-1]
+        first = jnp.where(core == 0, mine, other) * stored
         part = slice(n % 2 * rhs, (n % 2 + 1) * rhs)
-        right[slots, part] = shard[:stored]
-        left[slots, part] = -shard[stored:, :, pl.ds(start, half)]
-
-
-def products_kernel(stored, *refs):
+        right[pl.ds(first, stored), part] = shard[:stored]
+        left[pl.ds(first, stored), part] = -shard[stored:, :, pl.ds(start, half)]
+
+
+def products_kernel(stored, masks, *refs):
     shards, refs = refs[:-8], refs[-8:]
     home, rows, cols, out, left, right, result, sem = refs
-    stage(shards, left, right)
+    stage(masks, shards, left, right)
     mine = lax.axis_index("blk") * stored
     strips, per_strip = rows.shape
     chunks = strips * per_strip // CHUNK
@@ -127,7 +127,7 @@
         part = pl.ds(n * CHUNK, CHUNK)
         return pltpu.make_async_copy(result.at[part], out.at[part], sem.at[n])
 
-    def one_strip(strip, carry):
+    def one_strip(strip):
         for k in range(per_strip):
             a = left[jnp.bitwise_xor(home[rows[strip, k]], mine)]
             b = right[jnp.bitwise_xor(home[cols[strip, k]], mine)]
@@ -137,10 +137,9 @@
             result[strip * per_strip + k] = product.astype(jnp.bfloat16)
             if k % CHUNK == CHUNK - 1:
                 out_copy(strip * (per_strip // CHUNK) + k // CHUNK).start()
-        return carry
 
     for strip in range(strips):
-        one_strip(strip, 0)
+        one_strip(strip)
 
     def drain(n, carry):
         out_copy(n).wait()
@@ -149,14 +148,14 @@
     lax.fori_loop(0, chunks, drain, 0)
 
 
-def products(shards, index):
+def products(masks, shards, index):
     joined, rhs, width = shards[0].shape
     stored, half = joined // 2, width // 2
     slots = len(shards) // 2 * stored
     entries = index[1].size
     out = jax.ShapeDtypeStruct((entries, half, width), jnp.bfloat16)
     return pl.pallas_call(
-        functools.partial(products_kernel, stored),
+        functools.partial(products_kernel, stored, masks),
         out_shape=out,
         in_specs=[VMEM] * len(shards) + [SMEM] * 3,
         out_specs=ANY,
@@ -170,30 +169,33 @@
     )(*shards, *index)
 
 
-PLAN = ((6, 6), (2, 2), (1, 1), (3, 2), (7, 1), (4, 2), (5, 1))
+PLAN = ((0, 6, 4), (0, 2, 1), (0, 1, 2), (2, 1, 2), (1, 1, 2), (1, 2, 1), (5, 2, 1))
 
 
 def gathered(forward, adjoint, row_home, block_rows, block_cols):
     owners = lax.axis_size("blk")
 
-    def across(value, mask):
-        return lax.ppermute(value, "blk", [(i, i ^ mask) for i in range(owners)])
+    def across(value, *steps):
+        pairs = [(2 * i + c, 2 * (i ^ steps[c]) + c) for i in range(owners) for c in range(2)]
+        return lax.ppermute(value, ("blk", "rhs"), pairs)
 
     own, *index = load(forward, adjoint, (row_home, block_rows, block_cols))
-    held = {0: own}
-    for mask, via in PLAN:
-        held[mask] = across(held[mask ^ via], via)
+    held, masks = [own], [(0, 0)]
+    for source, first, second in PLAN:
+        held.append(across(held[source], first, second))
+        masks.append((masks[source][0] ^ first, masks[source][1] ^ second))
     shards = []
-    for j in range(owners):
-        shards += [held[j], lax.ppermute(held[j], "rhs", [(0, 1), (1, 0)])]
-    result = products(shards, index)
+    for v in held:
+        shards += [v, lax.ppermute(v, "rhs", [(0, 1), (1, 0)])]
+    result = products(masks, shards, index)
     return result.reshape(2, block_rows.shape[1], *result.shape[1:])
 
 
 def body(forward, adjoint, row_home, block_rows, block_cols):
     owners, stored = lax.axis_size("blk"), forward.shape[0]
     few = owners * stored <= 2 * block_rows.shape[1]
-    if few and owners == 8 and stored & (stored - 1) == 0 and block_rows.shape[1] % CHUNK == 0:
+    whole = owners == 8 and lax.axis_size("rhs") == 2 and stored & (stored - 1) == 0
+    if few and whole and block_rows.shape[1] % CHUNK == 0:
         return gathered(forward, adjoint, row_home, block_rows, block_cols)
     return tabled(forward, adjoint, row_home, block_rows, block_cols)
 

time: 24.5 us -> 24.3 us (level)
  waiting for transfers between devices: 7.37 us -> 8.08 us
  starting transfers between devices: 13.4 us -> 12.7 us
    ppermute x15, waiting for transfers between devices: 7.37 us -> 8.08 us  [the longest x7 6.79 us: across(): return lax.ppermute(value, ('blk', 'rhs'), pairs)]
    ppermute x15, starting transfers between devices: 13.4 us -> 12.7 us  [the longest x7 11.6 us: across(): return lax.ppermute(value, ('blk', 'rhs'), pairs)]
where the time goes in v5:
time: 24.3 us; the launch traced here: 24.1 us
  starting transfers between devices  12.7 us (52%)
  waiting for transfers between devices  8.08 us (33%)
  Pallas kernels  3.37 us (14%)
    ppermute x7, starting transfers between devices, across(): return lax.ppermute(value, ('blk', 'rhs'), pairs)  11.6 us
    ppermute x7, waiting for transfers between devices, across(): return lax.ppermute(value, ('blk', 'rhs'), pairs)  6.79 us
    pallas_call x1, Pallas kernels, products(): pl.pallas_call(functools.partial(products_kernel, stored, masks), out_sha...  2.5 us
    ppermute x8, waiting for transfers between devices, gathered(): shards += [v, lax.ppermute(v, 'rhs', [(0, 1), (1, 0)])]  1.29 us
    ppermute x8, starting transfers between devices, gathered(): shards += [v, lax.ppermute(v, 'rhs', [(0, 1), (1, 0)])]  1.05 us
    pallas_call x1, Pallas kernels, load(): pl.pallas_call(load_kernel, out_shape=[pltpu.VMEM((2 * a.shape[0],) + a.s...  0.87 us
  transfers between devices with their start and end apart: 15, of which 6 were waited for; matrix products, arithmetic and copies ran while one was open for 0% of the time, Pallas kernels for 0%

profile of v5, /device:TPU:0, one launch (start us, length us, event | category | flops | bytes accessed | tf_op | source)
XLA Modules:
  0.0 24.1 jit_solution(87789731076193221)
XLA Ops:
  0.0 0.9 %shard_map.55 = (bf16[16,16,256]{2,1,0:T(8,128)(2,1)S(1)}, s32[64]{0:T(128)S(4)}, s32[2,32]{1,0:T(2,128)S(4)}, s32[2,32]{1,0:T(2,128)S(4)}) custom-call(bf16[8,16,256]{2,1,0:T(8,128)(2,1)} %a.1, bf16[8,16,256]{2,1,0:T(8,128)(2,1)} %b.1, s32[64]{0:T(128)} %home.1, s32[2,32]{1,0:T(2,128)} %rows.1, s32[2,32]{1,0:T(2,128)} %cols.1), custom_call_target="tpu_custom_call" | custom-call | tf_op jit(solution)/shard_map/pallas_call | solution.py:94
  0.9 5.1 %collective-permute-start.1 = (bf16[16,16,256]{2,1,0:T(8,128)(2,1)S(1)}, bf16[16,16,256]{2,1,0:T(8,128)(2,1)S(1)}, u32[]{:S(2)}, u32[]{:S(2)}) collective-permute-start(bf16[16,16,256]{2,1,0:T(8,128)(2,1)S(1)} %get-tuple-element.9.refs_0_), channel_id=1, source_target_pairs={{0,12},{1,9},{2,14},{3,11},{4,8},{5,13},{6,10},{7,15},{8,4},{9,1},... | collective-permute-start | bytes 393224 | tf_op jit(solution)/shard_map/ppermute | solution.py:180
  6.0 1.5 %collective-permute-start.5 = (bf16[16,16,256]{2,1,0:T(8,128)(2,1)S(1)}, bf16[16,16,256]{2,1,0:T(8,128)(2,1)S(1)}, u32[]{:S(2)}, u32[]{:S(2)}) collective-permute-start(bf16[16,16,256]{2,1,0:T(8,128)(2,1)S(1)} %get-tuple-element.9.refs_0_), channel_id=1, source_target_pairs={{0,2},{1,5},{2,0},{3,7},{4,6},{5,1},{6,4},{7,3},{8,10},{9,13},{10,... | collective-permute-start | bytes 393224 | tf_op jit(solution)/shard_map/ppermute | solution.py:180
  7.5 0.0 collective-permute-start.3
  7.5 0.0 collective-permute-start
  7.5 2.9 %collective-permute-done.1.refs_2_ = bf16[16,16,256]{2,1,0:T(8,128)(2,1)S(1)} collective-permute-done((bf16[16,16,256]{2,1,0:T(8,128)(2,1)S(1)}, bf16[16,16,256]{2,1,0:T(8,128)(2,1)S(1)}, u32[]{:S(2)}, u32[]{:S(2)}) %collective-permute-start.1) | collective-permute-done | bytes 131104 | tf_op jit(solution)/shard_map/ppermute | solution.py:180
  10.4 1.7 %collective-permute-start.9 = (bf16[16,16,256]{2,1,0:T(8,128)(2,1)S(1)}, bf16[16,16,256]{2,1,0:T(8,128)(2,1)S(1)}, u32[]{:S(2)}, u32[]{:S(2)}) collective-permute-start(bf16[16,16,256]{2,1,0:T(8,128)(2,1)S(1)} %collective-permute-done.1.refs_2_), channel_id=1, source_target_pairs={{0,2},{1,5},{2,0},{3,7},{4,6},{5,1},{6,4},{7,3},{8,10},{9,13},{10,... | collective-permute-start | bytes 393224 | tf_op jit(solution)/shard_map/ppermute | solution.py:180
  12.0 0.0 collective-permute-done.5.refs_6_
  12.1 0.0 collective-permute-start.6
  12.1 0.4 %collective-permute-done.3.refs_4_ = bf16[16,16,256]{2,1,0:T(8,128)(2,1)S(1)} collective-permute-done((bf16[16,16,256]{2,1,0:T(8,128)(2,1)S(1)}, bf16[16,16,256]{2,1,0:T(8,128)(2,1)S(1)}, u32[]{:S(2)}, u32[]{:S(2)}) %collective-permute-start.3) | collective-permute-done | bytes 131104 | tf_op jit(solution)/shard_map/ppermute | solution.py:180
  12.5 0.9 %collective-permute-start.7 = (bf16[16,16,256]{2,1,0:T(8,128)(2,1)S(1)}, bf16[16,16,256]{2,1,0:T(8,128)(2,1)S(1)}, u32[]{:S(2)}, u32[]{:S(2)}) collective-permute-start(bf16[16,16,256]{2,1,0:T(8,128)(2,1)S(1)} %collective-permute-done.3.refs_4_), channel_id=1, source_target_pairs={{0,2},{1,5},{2,0},{3,7},{4,6},{5,1},{6,4},{7,3},{8,10},{9,13},{10,... | collective-permute-start | bytes 393224 | tf_op jit(solution)/shard_map/ppermute | solution.py:180
  13.3 0.4 %collective-permute-start.4 = (bf16[16,16,256]{2,1,0:T(8,128)(2,1)S(1)}, bf16[16,16,256]{2,1,0:T(8,128)(2,1)S(1)}, u32[]{:S(2)}, u32[]{:S(2)}) collective-permute-start(bf16[16,16,256]{2,1,0:T(8,128)(2,1)S(1)} %collective-permute-done.3.refs_4_), channel_id=1, source_target_pairs={{0,1},{1,0},{2,3},{3,2},{4,5},{5,4},{6,7},{7,6},{8,9},{9,8},{10,11... | collective-permute-start | bytes 393224 | tf_op jit(solution)/shard_map/ppermute | solution.py:189
  13.7 0.0 collective-permute-done.refs_1_
  13.7 0.8 %collective-permute-start.11 = (bf16[16,16,256]{2,1,0:T(8,128)(2,1)S(1)}, bf16[16,16,256]{2,1,0:T(8,128)(2,1)S(1)}, u32[]{:S(2)}, u32[]{:S(2)}) collective-permute-start(bf16[16,16,256]{2,1,0:T(8,128)(2,1)S(1)} %collective-permute-done.1.refs_2_), channel_id=1, source_target_pairs={{0,4},{1,3},{2,6},{3,1},{4,0},{5,7},{6,2},{7,5},{8,12},{9,11},{10,... | collective-permute-start | bytes 393224 | tf_op jit(solution)/shard_map/ppermute | solution.py:180
  14.5 0.8 %collective-permute-done.9.refs_10_ = bf16[16,16,256]{2,1,0:T(8,128)(2,1)S(1)} collective-permute-done((bf16[16,16,256]{2,1,0:T(8,128)(2,1)S(1)}, bf16[16,16,256]{2,1,0:T(8,128)(2,1)S(1)}, u32[]{:S(2)}, u32[]{:S(2)}) %collective-permute-start.9) | collective-permute-done | bytes 131104 | tf_op jit(solution)/shard_map/ppermute | solution.py:180
  15.3 1.7 %collective-permute-start.13 = (bf16[16,16,256]{2,1,0:T(8,128)(2,1)S(1)}, bf16[16,16,256]{2,1,0:T(8,128)(2,1)S(1)}, u32[]{:S(2)}, u32[]{:S(2)}) collective-permute-start(bf16[16,16,256]{2,1,0:T(8,128)(2,1)S(1)} %collective-permute-done.9.refs_10_), channel_id=1, source_target_pairs={{0,4},{1,3},{2,6},{3,1},{4,0},{5,7},{6,2},{7,5},{8,12},{9,11},{10,... | collective-permute-start | bytes 393224 | tf_op jit(solution)/shard_map/ppermute | solution.py:180
  17.0 0.0 collective-permute-done.6.refs_7_
  17.0 0.0 collective-permute-start.2
  17.0 1.5 %collective-permute-done.7.refs_8_ = bf16[16,16,256]{2,1,0:T(8,128)(2,1)S(1)} collective-permute-done((bf16[16,16,256]{2,1,0:T(8,128)(2,1)S(1)}, bf16[16,16,256]{2,1,0:T(8,128)(2,1)S(1)}, u32[]{:S(2)}, u32[]{:S(2)}) %collective-permute-start.7) | collective-permute-done | bytes 131104 | tf_op jit(solution)/shard_map/ppermute | solution.py:180
  18.5 0.0 collective-permute-start.10
  18.5 0.0 collective-permute-done.4.refs_5_
  18.5 0.5 %collective-permute-start.8 = (bf16[16,16,256]{2,1,0:T(8,128)(2,1)S(1)}, bf16[16,16,256]{2,1,0:T(8,128)(2,1)S(1)}, u32[]{:S(2)}, u32[]{:S(2)}) collective-permute-start(bf16[16,16,256]{2,1,0:T(8,128)(2,1)S(1)} %collective-permute-done.7.refs_8_), channel_id=1, source_target_pairs={{0,1},{1,0},{2,3},{3,2},{4,5},{5,4},{6,7},{7,6},{8,9},{9,8},{10,11... | collective-permute-start | bytes 393224 | tf_op jit(solution)/shard_map/ppermute | solution.py:189
  19.0 0.0 collective-permute-done.11.refs_12_
  19.0 0.1 collective-permute-start.12
  19.1 1.2 %collective-permute-done.13.refs_14_ = bf16[16,16,256]{2,1,0:T(8,128)(2,1)S(1)} collective-permute-done((bf16[16,16,256]{2,1,0:T(8,128)(2,1)S(1)}, bf16[16,16,256]{2,1,0:T(8,128)(2,1)S(1)}, u32[]{:S(2)}, u32[]{:S(2)}) %collective-permute-start.13) | collective-permute-done | bytes 131104 | tf_op jit(solution)/shard_map/ppermute | solution.py:180
  20.3 0.0 collective-permute-start.14
  20.3 0.0 collective-permute-done.2.refs_3_
  20.3 0.0 collective-permute-done.8.refs_9_
  20.4 0.0 collective-permute-done.12.refs_13_
  20.4 0.0 collective-permute-done.10.refs_11_
  20.4 1.3 %collective-permute-done.14.refs_15_ = bf16[16,16,256]{2,1,0:T(8,128)(2,1)S(1)} collective-permute-done((bf16[16,16,256]{2,1,0:T(8,128)(2,1)S(1)}, bf16[16,16,256]{2,1,0:T(8,128)(2,1)S(1)}, u32[]{:S(2)}, u32[]{:S(2)}) %collective-permute-start.14) | collective-permute-done | bytes 131104 | tf_op jit(solution)/shard_map/ppermute | solution.py:189
  21.6 2.5 %shard_map.56 = bf16[64,128,256]{2,1,0:T(8,128)(2,1)} custom-call(bf16[16,16,256]{2,1,0:T(8,128)(2,1)S(1)} %get-tuple-element.9.refs_0_, bf16[16,16,256]{2,1,0:T(8,128)(2,1)S(1)} %collective-permute-done.refs_1_, bf16[16,16,256]{2,1,0:T(8,128)(2,1)S(1)} %collective-permute-done.1.refs_2_, bf16[16,16,256]{2,1,0:T(8,128)(2,1)S(1)} %collective-permute-done.2.refs_3_, ...), custom_call_target="tpu_custom_call" | custom-call | tf_op jit(solution)/shard_map/pallas_call | solution.py:157
Async XLA Ops:
  0.9 9.5 %collective-permute-start.1 = (bf16[16,16,256]{2,1,0:T(8,128)(2,1)S(1)}, bf16[16,16,256]{2,1,0:T(8,128)(2,1)S(1)}, u32[]{:S(2)}, u32[]{:S(2)}) collective-permute-start(bf16[16,16,256]{2,1,0:T(8,128)(2,1)S(1)} %get-tuple-element.9.refs_0_), channel_id=1, source_target_pairs={{0,12},{1,9},{2,14},{3,11},{4,8},{5,13},{6,10},{7,15},{8,4},{9,1},... | collective-permute-start | bytes 393224 | tf_op jit(solution)/shard_map/ppermute | solution.py:180
  6.0 6.1 %collective-permute-start.5 = (bf16[16,16,256]{2,1,0:T(8,128)(2,1)S(1)}, bf16[16,16,256]{2,1,0:T(8,128)(2,1)S(1)}, u32[]{:S(2)}, u32[]{:S(2)}) collective-permute-start(bf16[16,16,256]{2,1,0:T(8,128)(2,1)S(1)} %get-tuple-element.9.refs_0_), channel_id=1, source_target_pairs={{0,2},{1,5},{2,0},{3,7},{4,6},{5,1},{6,4},{7,3},{8,10},{9,13},{10,... | collective-permute-start | bytes 393224 | tf_op jit(solution)/shard_map/ppermute | solution.py:180
  7.5 5.0 %collective-permute-start.3 = (bf16[16,16,256]{2,1,0:T(8,128)(2,1)S(1)}, bf16[16,16,256]{2,1,0:T(8,128)(2,1)S(1)}, u32[]{:S(2)}, u32[]{:S(2)}) collective-permute-start(bf16[16,16,256]{2,1,0:T(8,128)(2,1)S(1)} %get-tuple-element.9.refs_0_), channel_id=1, source_target_pairs={{0,4},{1,3},{2,6},{3,1},{4,0},{5,7},{6,2},{7,5},{8,12},{9,11},{10,... | collective-permute-start | bytes 393224 | tf_op jit(solution)/shard_map/ppermute | solution.py:180
  7.5 6.3 %collective-permute-start = (bf16[16,16,256]{2,1,0:T(8,128)(2,1)S(1)}, bf16[16,16,256]{2,1,0:T(8,128)(2,1)S(1)}, u32[]{:S(2)}, u32[]{:S(2)}) collective-permute-start(bf16[16,16,256]{2,1,0:T(8,128)(2,1)S(1)} %get-tuple-element.9.refs_0_), channel_id=1, source_target_pairs={{0,1},{1,0},{2,3},{3,2},{4,5},{5,4},{6,7},{7,6},{8,9},{9,8},{10,11... | collective-permute-start | bytes 393224 | tf_op jit(solution)/shard_map/ppermute | solution.py:189
  10.4 5.0 %collective-permute-start.9 = (bf16[16,16,256]{2,1,0:T(8,128)(2,1)S(1)}, bf16[16,16,256]{2,1,0:T(8,128)(2,1)S(1)}, u32[]{:S(2)}, u32[]{:S(2)}) collective-permute-start(bf16[16,16,256]{2,1,0:T(8,128)(2,1)S(1)} %collective-permute-done.1.refs_2_), channel_id=1, source_target_pairs={{0,2},{1,5},{2,0},{3,7},{4,6},{5,1},{6,4},{7,3},{8,10},{9,13},{10,... | collective-permute-start | bytes 393224 | tf_op jit(solution)/shard_map/ppermute | solution.py:180
  12.1 4.9 %collective-permute-start.6 = (bf16[16,16,256]{2,1,0:T(8,128)(2,1)S(1)}, bf16[16,16,256]{2,1,0:T(8,128)(2,1)S(1)}, u32[]{:S(2)}, u32[]{:S(2)}) collective-permute-start(bf16[16,16,256]{2,1,0:T(8,128)(2,1)S(1)} %collective-permute-done.5.refs_6_), channel_id=1, source_target_pairs={{0,1},{1,0},{2,3},{3,2},{4,5},{5,4},{6,7},{7,6},{8,9},{9,8},{10,11... | collective-permute-start | bytes 393224 | tf_op jit(solution)/shard_map/ppermute | solution.py:189
  12.5 6.0 %collective-permute-start.7 = (bf16[16,16,256]{2,1,0:T(8,128)(2,1)S(1)}, bf16[16,16,256]{2,1,0:T(8,128)(2,1)S(1)}, u32[]{:S(2)}, u32[]{:S(2)}) collective-permute-start(bf16[16,16,256]{2,1,0:T(8,128)(2,1)S(1)} %collective-permute-done.3.refs_4_), channel_id=1, source_target_pairs={{0,2},{1,5},{2,0},{3,7},{4,6},{5,1},{6,4},{7,3},{8,10},{9,13},{10,... | collective-permute-start | bytes 393224 | tf_op jit(solution)/shard_map/ppermute | solution.py:180
  13.3 5.2 %collective-permute-start.4 = (bf16[16,16,256]{2,1,0:T(8,128)(2,1)S(1)}, bf16[16,16,256]{2,1,0:T(8,128)(2,1)S(1)}, u32[]{:S(2)}, u32[]{:S(2)}) collective-permute-start(bf16[16,16,256]{2,1,0:T(8,128)(2,1)S(1)} %collective-permute-done.3.refs_4_), channel_id=1, source_target_pairs={{0,1},{1,0},{2,3},{3,2},{4,5},{5,4},{6,7},{7,6},{8,9},{9,8},{10,11... | collective-permute-start | bytes 393224 | tf_op jit(solution)/shard_map/ppermute | solution.py:189
  13.7 5.3 %collective-permute-start.11 = (bf16[16,16,256]{2,1,0:T(8,128)(2,1)S(1)}, bf16[16,16,256]{2,1,0:T(8,128)(2,1)S(1)}, u32[]{:S(2)}, u32[]{:S(2)}) collective-permute-start(bf16[16,16,256]{2,1,0:T(8,128)(2,1)S(1)} %collective-permute-done.1.refs_2_), channel_id=1, source_target_pairs={{0,4},{1,3},{2,6},{3,1},{4,0},{5,7},{6,2},{7,5},{8,12},{9,11},{10,... | collective-permute-start | bytes 393224 | tf_op jit(solution)/shard_map/ppermute | solution.py:180
  15.3 5.0 %collective-permute-start.13 = (bf16[16,16,256]{2,1,0:T(8,128)(2,1)S(1)}, bf16[16,16,256]{2,1,0:T(8,128)(2,1)S(1)}, u32[]{:S(2)}, u32[]{:S(2)}) collective-permute-start(bf16[16,16,256]{2,1,0:T(8,128)(2,1)S(1)} %collective-permute-done.9.refs_10_), channel_id=1, source_target_pairs={{0,4},{1,3},{2,6},{3,1},{4,0},{5,7},{6,2},{7,5},{8,12},{9,11},{10,... | collective-permute-start | bytes 393224 | tf_op jit(solution)/shard_map/ppermute | solution.py:180
  17.0 3.4 %collective-permute-start.2 = (bf16[16,16,256]{2,1,0:T(8,128)(2,1)S(1)}, bf16[16,16,256]{2,1,0:T(8,128)(2,1)S(1)}, u32[]{:S(2)}, u32[]{:S(2)}) collective-permute-start(bf16[16,16,256]{2,1,0:T(8,128)(2,1)S(1)} %collective-permute-done.1.refs_2_), channel_id=1, source_target_pairs={{0,1},{1,0},{2,3},{3,2},{4,5},{5,4},{6,7},{7,6},{8,9},{9,8},{10,11... | collective-permute-start | bytes 393224 | tf_op jit(solution)/shard_map/ppermute | solution.py:189
  18.5 1.9 %collective-permute-start.10 = (bf16[16,16,256]{2,1,0:T(8,128)(2,1)S(1)}, bf16[16,16,256]{2,1,0:T(8,128)(2,1)S(1)}, u32[]{:S(2)}, u32[]{:S(2)}) collective-permute-start(bf16[16,16,256]{2,1,0:T(8,128)(2,1)S(1)} %collective-permute-done.9.refs_10_), channel_id=1, source_target_pairs={{0,1},{1,0},{2,3},{3,2},{4,5},{5,4},{6,7},{7,6},{8,9},{9,8},{10,11... | collective-permute-start | bytes 393224 | tf_op jit(solution)/shard_map/ppermute | solution.py:189
  18.5 1.9 %collective-permute-start.8 = (bf16[16,16,256]{2,1,0:T(8,128)(2,1)S(1)}, bf16[16,16,256]{2,1,0:T(8,128)(2,1)S(1)}, u32[]{:S(2)}, u32[]{:S(2)}) collective-permute-start(bf16[16,16,256]{2,1,0:T(8,128)(2,1)S(1)} %collective-permute-done.7.refs_8_), channel_id=1, source_target_pairs={{0,1},{1,0},{2,3},{3,2},{4,5},{5,4},{6,7},{7,6},{8,9},{9,8},{10,11... | collective-permute-start | bytes 393224 | tf_op jit(solution)/shard_map/ppermute | solution.py:189
  19.0 1.4 %collective-permute-start.12 = (bf16[16,16,256]{2,1,0:T(8,128)(2,1)S(1)}, bf16[16,16,256]{2,1,0:T(8,128)(2,1)S(1)}, u32[]{:S(2)}, u32[]{:S(2)}) collective-permute-start(bf16[16,16,256]{2,1,0:T(8,128)(2,1)S(1)} %collective-permute-done.11.refs_12_), channel_id=1, source_target_pairs={{0,1},{1,0},{2,3},{3,2},{4,5},{5,4},{6,7},{7,6},{8,9},{9,8},{10,11... | collective-permute-start | bytes 393224 | tf_op jit(solution)/shard_map/ppermute | solution.py:189
  20.3 1.3 %collective-permute-start.14 = (bf16[16,16,256]{2,1,0:T(8,128)(2,1)S(1)}, bf16[16,16,256]{2,1,0:T(8,128)(2,1)S(1)}, u32[]{:S(2)}, u32[]{:S(2)}) collective-permute-start(bf16[16,16,256]{2,1,0:T(8,128)(2,1)S(1)} %collective-permute-done.13.refs_14_), channel_id=1, source_target_pairs={{0,1},{1,0},{2,3},{3,2},{4,5},{5,4},{6,7},{7,6},{8,9},{9,8},{10,11... | collective-permute-start | bytes 393224 | tf_op jit(solution)/shard_map/ppermute | solution.py:189
